TPU v7x, 256 devices: a whole 4x4x8 slice. The times are simulated.
256 devices in a mesh: pp: 8 (over y, x_hi), ep: 32 (over z, x_lo, core).
Axes of the slice: x: 4 (x_hi: 2, x_lo: 2; x = x_hi * 2 + x_lo), y: 4, z: 8, core: 2. Of those that a mesh axis runs over, the one named last changes fastest.
Arguments:
- forward_in: bfloat16 [8, 4096, 7168], P('pp', 'ep'), may hold values from -4 to 4
- grad_in: bfloat16 [8, 4096, 7168], P('pp', 'ep'), may hold values from -4 to 4
- routes: int32 [8, 2, 2, 4096, 8], P('pp', None, None, 'ep'), may hold values from 0 to 255, as said below
- gate_weights: float32 [8, 2, 2, 4096, 8], P('pp', None, None, 'ep'), may hold values from 0.1 to 1
- saved_preact: bfloat16 [8, 2, 32, 32, 5, 256], P('pp', None, 'ep'), may hold values from -6 to 6
- gate_up: bfloat16 [8, 32, 7168, 256], P('pp', 'ep'), may hold values from -0.0625 to 0.0625
- down_proj: bfloat16 [8, 32, 128, 7168], P('pp', 'ep'), may hold values from -0.125 to 0.125
Outputs:
- forward_out: bfloat16 [8, 4096, 7168], P('pp', 'ep')
- grad_out: bfloat16 [8, 4096, 7168], P('pp', 'ep')
Inputs may be any that keep to these rules, and one draw needn't show every extreme that they name: `routes`: each row names 8 different experts. In each aligned block of 128 rows (the rows of one device), each expert below 2 is named by 2 to 5 rows; for every section, segment and stream one of these experts is named by exactly 5 rows in every block, and each of them by exactly 5 rows in at least one block.
All inputs are finite; a program needn't handle non-finite values.
Results may differ from a plain program's by a relative error of at most 0.0034.
Values may be sent and summed in bfloat16 or wider, within the bound.
A program may use at most 128 MiB of HBM per device.

v0:
```python
import jax
import jax.numpy as jnp
from jax import lax
from jax.sharding import PartitionSpec as P

EXP_SEC = 2
SEGMENTS = 2


def passed_along(value, axis, steps):
    count = lax.axis_size(axis)
    pairs = [(source, (source + steps) % count) for source in range(count)]
    return lax.ppermute(value, axis, pairs)


def slot_tables(expert_ids, weights, experts_here, capacity):
    labels = jnp.arange(experts_here, dtype=jnp.int32)
    is_named = expert_ids[:, :, None] == labels[None, None, :]
    member = jnp.any(is_named, axis=1)
    scales = jnp.sum(
        jnp.where(is_named, weights[:, :, None], jnp.zeros_like(weights[:, :, None])), axis=1
    )
    slot_rank = jnp.cumsum(member.astype(jnp.int32), axis=0) - 1
    places = jnp.arange(capacity, dtype=jnp.int32)
    onehot = member[:, :, None] & (slot_rank[:, :, None] == places[None, None, :])
    return (onehot, scales)


def pack_rows(onehot, tokens):
    return jnp.einsum(
        "tec,td->ecd", onehot.astype(jnp.bfloat16), tokens, preferred_element_type=jnp.float32
    ).astype(jnp.bfloat16)


def spread_rows(onehot, scales, totals, inputs):
    combine = (onehot.astype(jnp.float32) * scales[:, :, None]).reshape(onehot.shape[0], -1)
    flat_totals = totals.reshape(combine.shape[1], -1)
    summed = jnp.dot(
        combine, flat_totals, precision=lax.Precision.HIGHEST, preferred_element_type=jnp.float32
    )
    return (summed + inputs.astype(jnp.float32)).astype(jnp.bfloat16)


def expert_forward(routed, w_in, w_out):
    sources, capacity, model_width = routed.shape
    flat_rows = routed.reshape(sources * capacity, model_width)
    hidden_width = w_out.shape[0]
    activation = jnp.dot(flat_rows, w_in, preferred_element_type=jnp.float32)
    hidden = (jax.nn.silu(activation[:, :hidden_width]) * activation[:, hidden_width:]).astype(
        jnp.bfloat16
    )
    result = jnp.dot(hidden, w_out, preferred_element_type=jnp.float32).astype(jnp.bfloat16)
    return result.reshape(sources, capacity, model_width)


def expert_backward(routed, stored, w_in, w_out):
    sources, capacity, model_width = routed.shape
    flat_rows = routed.reshape(sources * capacity, model_width)
    hidden_width = w_out.shape[0]
    preact = stored.reshape(sources * capacity, 2 * hidden_width).astype(jnp.float32)
    gate_pre = preact[:, :hidden_width]
    up_pre = preact[:, hidden_width:]
    grad_hidden = lax.dot_general(
        flat_rows, w_out, (((1,), (1,)), ((), ())), preferred_element_type=jnp.float32
    )
    sigmoid_gate = jax.nn.sigmoid(gate_pre)
    grad_gate = grad_hidden * up_pre * sigmoid_gate * (1.0 + gate_pre * (1.0 - sigmoid_gate))
    grad_up = grad_hidden * gate_pre * sigmoid_gate
    grad_pair = jnp.concatenate([grad_gate, grad_up], axis=1).astype(jnp.bfloat16)
    returned = lax.dot_general(
        grad_pair, w_in, (((1,), (1,)), ((), ())), preferred_element_type=jnp.float32
    )
    return returned.astype(jnp.bfloat16).reshape(sources, capacity, model_width)


def local(forward_in, grad_in, routes, gate_weights, saved_preact, gate_up, down_proj):
    shards = lax.axis_size("ep")
    split_ways = shards // EXP_SEC
    capacity = saved_preact.shape[4]
    w_in = gate_up[0, 0]
    w_out = down_proj[0, 0]
    model_width = w_out.shape[1]

    def send_rows(packed):
        outgoing = jnp.repeat(packed, split_ways, axis=0)
        return lax.all_to_all(outgoing, "ep", split_axis=0, concat_axis=0, tiled=True)

    def return_sums(partial_value):
        returned = lax.all_to_all(partial_value, "ep", split_axis=0, concat_axis=0, tiled=True)
        return jnp.sum(
            returned.astype(jnp.float32).reshape(EXP_SEC, split_ways, capacity, model_width), axis=1
        )

    moving = forward_in[0]
    falling = grad_in[0]
    for step_index in range(SEGMENTS):
        moving = passed_along(moving, "pp", 1)
        falling = passed_along(falling, "pp", -1)
        ahead, ahead_scale = slot_tables(
            routes[0, step_index, 0], gate_weights[0, step_index, 0], EXP_SEC, capacity
        )
        behind, behind_scale = slot_tables(
            routes[0, step_index, 1], gate_weights[0, step_index, 1], EXP_SEC, capacity
        )
        routed_ahead = send_rows(pack_rows(ahead, moving))
        totals_ahead = return_sums(expert_forward(routed_ahead, w_in, w_out))
        routed_behind = send_rows(pack_rows(behind, falling))
        totals_behind = return_sums(
            expert_backward(routed_behind, saved_preact[0, step_index, 0], w_in, w_out)
        )
        moving = spread_rows(ahead, ahead_scale, totals_ahead, moving)
        falling = spread_rows(behind, behind_scale, totals_behind, falling)
    return (moving[None], falling[None])


def solution(mesh):
    in_specs = (
        P("pp", "ep", None),
        P("pp", "ep", None),
        P("pp", None, None, "ep", None),
        P("pp", None, None, "ep", None),
        P("pp", None, "ep", None, None, None),
        P("pp", "ep", None, None),
        P("pp", "ep", None, None),
    )
    out_specs = (P("pp", "ep", None), P("pp", "ep", None))
    return jax.shard_map(local, mesh=mesh, in_specs=in_specs, out_specs=out_specs, check_vma=False)
```

profile of v0, /device:TPU:1, one launch (start us, length us, event | category | flops | bytes accessed | tf_op | source)
XLA Modules:
  0.0 812.3 jit_solution(8393806275841806046)
XLA Ops:
  0.6 6.1 collective-permute-start.2
  7.9 37.9 %collective-permute-done.2 = bf16[128,7168]{1,0:T(8,128)(2,1)} collective-permute-done((bf16[128,7168]{1,0:T(8,128)(2,1)}, bf16[128,7168]{1,0:T(8,128)(2,1)}, u32[]{:S(2)}, u32[]{:S(2)}) %collective-permute-start.2) | collective-permute-done | bytes 1835040 | tf_op jit(solution)/shard_map/ppermute | solution.py:13
  49.8 10.2 %all-to-all-start.4 = ((bf16[32,5,7168]{2,1,0:T(8,128)(2,1)}), bf16[32,5,7168]{2,1,0:T(8,128)(2,1)}, u32[]{:S(2)}, u32[]{:S(2)}) async-start(bf16[32,5,7168]{2,1,0:T(8,128)(2,1)} %bitcast.98), calls=%async_computation.4 | async-start | bytes 7340032 | tf_op jit(solution)/shard_map/all_to_all | solution.py:86
  63.3 82.8 %collective-permute-done = bf16[128,7168]{1,0:T(8,128)(2,1)} collective-permute-done((bf16[128,7168]{1,0:T(8,128)(2,1)}, bf16[128,7168]{1,0:T(8,128)(2,1)}, u32[]{:S(2)}, u32[]{:S(2)}) %collective-permute-start) | collective-permute-done | bytes 1835040 | tf_op jit(solution)/shard_map/ppermute | solution.py:13
  150.3 8.3 %all-to-all-start = ((bf16[32,5,7168]{2,1,0:T(8,128)(2,1)}), bf16[32,5,7168]{2,1,0:T(8,128)(2,1)}, u32[]{:S(2)}, u32[]{:S(2)}) async-start(bf16[32,5,7168]{2,1,0:T(8,128)(2,1)} %bitcast.97), calls=%async_computation | async-start | bytes 7340032 | tf_op jit(solution)/shard_map/all_to_all | solution.py:86
  158.8 4.6 reshape.139
  173.5 70.5 %all-to-all-done = bf16[32,5,7168]{2,1,0:T(8,128)(2,1)} async-done(((bf16[32,5,7168]{2,1,0:T(8,128)(2,1)}), bf16[32,5,7168]{2,1,0:T(8,128)(2,1)}, u32[]{:S(2)}, u32[]{:S(2)}) %all-to-all-start) | async-done | bytes 2293792 | tf_op jit(solution)/shard_map/all_to_all | solution.py:86
  244.0 4.9 all-to-all-start.5
  248.9 4.6 reshape.129
  263.7 70.7 %all-to-all-done.5 = bf16[32,5,7168]{2,1,0:T(8,128)(2,1)} async-done(((bf16[32,5,7168]{2,1,0:T(8,128)(2,1)}), bf16[32,5,7168]{2,1,0:T(8,128)(2,1)}, u32[]{:S(2)}, u32[]{:S(2)}) %all-to-all-start.5) | async-done | bytes 2293792 | tf_op jit(solution)/shard_map/all_to_all | solution.py:89
  334.3 4.9 all-to-all-start.1
  342.1 5.5 add_convert_fusion.1
  348.7 71.0 %collective-permute-done.3 = bf16[128,7168]{1,0:T(8,128)(2,1)} collective-permute-done((bf16[128,7168]{1,0:T(8,128)(2,1)}, bf16[128,7168]{1,0:T(8,128)(2,1)}, u32[]{:S(2)}, u32[]{:S(2)}) %collective-permute-start.3) | collective-permute-done | bytes 1835040 | tf_op jit(solution)/shard_map/ppermute | solution.py:13
  427.0 5.6 all-to-all-start.6
  435.5 5.5 add_convert_fusion.3
  443.5 76.5 %collective-permute-done.1 = bf16[128,7168]{1,0:T(8,128)(2,1)} collective-permute-done((bf16[128,7168]{1,0:T(8,128)(2,1)}, bf16[128,7168]{1,0:T(8,128)(2,1)}, u32[]{:S(2)}, u32[]{:S(2)}) %collective-permute-start.1) | collective-permute-done | bytes 1835040 | tf_op jit(solution)/shard_map/ppermute | solution.py:13
  524.2 8.2 %all-to-all-start.2 = ((bf16[32,5,7168]{2,1,0:T(8,128)(2,1)}), bf16[32,5,7168]{2,1,0:T(8,128)(2,1)}, u32[]{:S(2)}, u32[]{:S(2)}) async-start(bf16[32,5,7168]{2,1,0:T(8,128)(2,1)} %bitcast.99), calls=%async_computation.2 | async-start | bytes 7340032 | tf_op jit(solution)/shard_map/all_to_all | solution.py:86
  547.3 70.5 %all-to-all-done.2 = bf16[32,5,7168]{2,1,0:T(8,128)(2,1)} async-done(((bf16[32,5,7168]{2,1,0:T(8,128)(2,1)}), bf16[32,5,7168]{2,1,0:T(8,128)(2,1)}, u32[]{:S(2)}, u32[]{:S(2)}) %all-to-all-start.2) | async-done | bytes 2293792 | tf_op jit(solution)/shard_map/all_to_all | solution.py:86
  617.8 4.9 all-to-all-start.7
  637.5 70.6 %all-to-all-done.7 = bf16[32,5,7168]{2,1,0:T(8,128)(2,1)} async-done(((bf16[32,5,7168]{2,1,0:T(8,128)(2,1)}), bf16[32,5,7168]{2,1,0:T(8,128)(2,1)}, u32[]{:S(2)}, u32[]{:S(2)}) %all-to-all-start.7) | async-done | bytes 2293792 | tf_op jit(solution)/shard_map/all_to_all | solution.py:89
  708.1 4.9 all-to-all-start.3
  715.9 82.6 %all-to-all-done.3 = bf16[32,5,7168]{2,1,0:T(8,128)(2,1)} async-done(((bf16[32,5,7168]{2,1,0:T(8,128)(2,1)}), bf16[32,5,7168]{2,1,0:T(8,128)(2,1)}, u32[]{:S(2)}, u32[]{:S(2)}) %all-to-all-start.3) | async-done | bytes 2293792 | tf_op jit(solution)/shard_map/all_to_all | solution.py:89
  801.3 5.5 fusion.7
  806.8 5.5 fusion.6
  (76 shorter events, 89.2 us)
Async XLA Ops:
  0.6 162.8 %copy-start = (bf16[1,1,128,7168]{3,2,1,0:T(8,128)(2,1)S(1)}, bf16[1,1,128,7168]{3,2,1,0:T(8,128)(2,1)}, u32[]{:S(2)}) copy-start(bf16[1,1,128,7168]{3,2,1,0:T(8,128)(2,1)} %param.13) | copy-start | bytes 5505028
  0.6 45.1 %collective-permute-start.2 = (bf16[128,7168]{1,0:T(8,128)(2,1)}, bf16[128,7168]{1,0:T(8,128)(2,1)}, u32[]{:S(2)}, u32[]{:S(2)}) collective-permute-start(bf16[128,7168]{1,0:T(8,128)(2,1)} %bitcast.100), channel_id=1, source_target_pairs={{0,224},{32,0},{64,32},{96,64},{128,96},{160,128},{192,160},{224,1... | collective-permute-start | bytes 5505032 | tf_op jit(solution)/shard_map/ppermute | solution.py:13
  49.8 98.2 %all-to-all-start.4 = ((bf16[32,5,7168]{2,1,0:T(8,128)(2,1)}), bf16[32,5,7168]{2,1,0:T(8,128)(2,1)}, u32[]{:S(2)}, u32[]{:S(2)}) async-start(bf16[32,5,7168]{2,1,0:T(8,128)(2,1)} %bitcast.98), calls=%async_computation.4 | async-start | bytes 7340032 | tf_op jit(solution)/shard_map/all_to_all | solution.py:86
  60.1 86.1 %collective-permute-start = (bf16[128,7168]{1,0:T(8,128)(2,1)}, bf16[128,7168]{1,0:T(8,128)(2,1)}, u32[]{:S(2)}, u32[]{:S(2)}) collective-permute-start(bf16[128,7168]{1,0:T(8,128)(2,1)} %bitcast.101), channel_id=1, source_target_pairs={{0,32},{32,64},{64,96},{96,128},{128,160},{160,192},{192,224},{224... | collective-permute-start | bytes 5505032 | tf_op jit(solution)/shard_map/ppermute | solution.py:13
  150.3 8.3 %copy-start.3 = (bf16[1,2,1,32,5,256]{5,3,4,2,1,0:T(8,128)(2,1)S(1)}, bf16[1,2,1,32,5,256]{5,3,4,2,1,0:T(8,128)(2,1)}, u32[]{:S(2)}) copy-start(bf16[1,2,1,32,5,256]{5,3,4,2,1,0:T(8,128)(2,1)} %param.11) | copy-start | bytes 491524
  150.3 93.7 %all-to-all-start = ((bf16[32,5,7168]{2,1,0:T(8,128)(2,1)}), bf16[32,5,7168]{2,1,0:T(8,128)(2,1)}, u32[]{:S(2)}, u32[]{:S(2)}) async-start(bf16[32,5,7168]{2,1,0:T(8,128)(2,1)} %bitcast.97), calls=%async_computation | async-start | bytes 7340032 | tf_op jit(solution)/shard_map/all_to_all | solution.py:86
  163.4 2.7 copy-start.1
  244.0 90.3 %all-to-all-start.5 = ((bf16[32,5,7168]{2,1,0:T(8,128)(2,1)}), bf16[32,5,7168]{2,1,0:T(8,128)(2,1)}, u32[]{:S(2)}, u32[]{:S(2)}) async-start(bf16[32,5,7168]{2,1,0:T(8,128)(2,1)} %reshape.140), calls=%async_computation.5 | async-start | bytes 7340032 | tf_op jit(solution)/shard_map/all_to_all | solution.py:89
  263.7 75.5 %copy-start.4 = (f32[1,2,2,128,8]{3,4,2,1,0:T(8,128)S(1)}, f32[1,2,2,128,8]{3,4,2,1,0:T(8,128)}, u32[]{:S(2)}) copy-start(f32[1,2,2,128,8]{3,4,2,1,0:T(8,128)} %param.10) | copy-start | bytes 49156
  334.3 90.3 %all-to-all-start.1 = ((bf16[32,5,7168]{2,1,0:T(8,128)(2,1)}), bf16[32,5,7168]{2,1,0:T(8,128)(2,1)}, u32[]{:S(2)}, u32[]{:S(2)}) async-start(bf16[32,5,7168]{2,1,0:T(8,128)(2,1)} %reshape.130), calls=%async_computation.1 | async-start | bytes 7340032 | tf_op jit(solution)/shard_map/all_to_all | solution.py:89
  347.6 72.1 %collective-permute-start.3 = (bf16[128,7168]{1,0:T(8,128)(2,1)}, bf16[128,7168]{1,0:T(8,128)(2,1)}, u32[]{:S(2)}, u32[]{:S(2)}) collective-permute-start(bf16[128,7168]{1,0:T(8,128)(2,1)} %add_convert_fusion.1), channel_id=1, source_target_pairs={{0,224},{32,0},{64,32},{96,64},{128,96},{160,128},{192,160},{224,1... | collective-permute-start | bytes 5505032 | tf_op jit(solution)/shard_map/ppermute | solution.py:13
  427.0 94.9 %all-to-all-start.6 = ((bf16[32,5,7168]{2,1,0:T(8,128)(2,1)}), bf16[32,5,7168]{2,1,0:T(8,128)(2,1)}, u32[]{:S(2)}, u32[]{:S(2)}) async-start(bf16[32,5,7168]{2,1,0:T(8,128)(2,1)} %bitcast.96), calls=%async_computation.6 | async-start | bytes 7340032 | tf_op jit(solution)/shard_map/all_to_all | solution.py:86
  441.0 79.0 %collective-permute-start.1 = (bf16[128,7168]{1,0:T(8,128)(2,1)}, bf16[128,7168]{1,0:T(8,128)(2,1)}, u32[]{:S(2)}, u32[]{:S(2)}) collective-permute-start(bf16[128,7168]{1,0:T(8,128)(2,1)} %add_convert_fusion.3), channel_id=1, source_target_pairs={{0,32},{32,64},{64,96},{96,128},{128,160},{160,192},{192,224},{224... | collective-permute-start | bytes 5505032 | tf_op jit(solution)/shard_map/ppermute | solution.py:13
  524.2 93.6 %all-to-all-start.2 = ((bf16[32,5,7168]{2,1,0:T(8,128)(2,1)}), bf16[32,5,7168]{2,1,0:T(8,128)(2,1)}, u32[]{:S(2)}, u32[]{:S(2)}) async-start(bf16[32,5,7168]{2,1,0:T(8,128)(2,1)} %bitcast.99), calls=%async_computation.2 | async-start | bytes 7340032 | tf_op jit(solution)/shard_map/all_to_all | solution.py:86
  537.2 2.7 copy-start.2
  617.8 90.3 %all-to-all-start.7 = ((bf16[32,5,7168]{2,1,0:T(8,128)(2,1)}), bf16[32,5,7168]{2,1,0:T(8,128)(2,1)}, u32[]{:S(2)}, u32[]{:S(2)}) async-start(bf16[32,5,7168]{2,1,0:T(8,128)(2,1)} %reshape.145), calls=%async_computation.7 | async-start | bytes 7340032 | tf_op jit(solution)/shard_map/all_to_all | solution.py:89
  708.1 90.3 %all-to-all-start.3 = ((bf16[32,5,7168]{2,1,0:T(8,128)(2,1)}), bf16[32,5,7168]{2,1,0:T(8,128)(2,1)}, u32[]{:S(2)}, u32[]{:S(2)}) async-start(bf16[32,5,7168]{2,1,0:T(8,128)(2,1)} %reshape.135), calls=%async_computation.3 | async-start | bytes 7340032 | tf_op jit(solution)/shard_map/all_to_all | solution.py:89
where the time goes:
time: 814 us; the launch traced here: 812 us
  waiting for transfers between devices  636 us (78%)
  starting transfers between devices  63.6 us (8%)
  matrix products  51.4 us (6%)
  local copies, waits for them, and re-layouts  47.9 us (6%)
  other arithmetic  12.3 us (2%)
    ppermute x4, waiting for transfers between devices, passed_along(): return lax.ppermute(value, axis, pairs)  268 us
    all_to_all x4, waiting for transfers between devices, return_sums(): lax.all_to_all(partial_value, 'ep', split_axis=0, concat_axis=0, tiled=True)  227 us
    all_to_all x4, waiting for transfers between devices, send_rows(): lax.all_to_all(outgoing, 'ep', split_axis=0, concat_axis=0, tiled=True)  141 us
    all_to_all x4, starting transfers between devices, send_rows(): lax.all_to_all(outgoing, 'ep', split_axis=0, concat_axis=0, tiled=True)  32.3 us
    dot_general x4, matrix products, spread_rows(): jnp.dot(combine, flat_totals, precision=lax.Precision.HIGHEST, preferred_...  21.9 us
    all_to_all x4, starting transfers between devices, return_sums(): lax.all_to_all(partial_value, 'ep', split_axis=0, concat_axis=0, tiled=True)  19.5 us
  transfers between devices with their start and end apart: 12, of which 10 were waited for; matrix products, arithmetic and copies ran while one was open for 11% of the time, Pallas kernels for 0%

commit v1 on v0

v1 whole, which is shorter than its diff:
```python
import functools

import jax
import jax.numpy as jnp
from jax import lax
from jax.experimental import pallas as pl
from jax.experimental.pallas import tpu as pltpu
from jax.sharding import PartitionSpec as P

EXP_SEC = 2
SEGMENTS = 2
CAP = 5
MESH = pl.DeviceIdType.MESH

HALF = 3584
LANES = 1280
PARTS = ((0, 1280), (1280, 1152), (2432, 1152))
PART_ROWS = ((0, 1, 2, 3, 4), (8, 9, 10, 11, 12), (5, 6, 7, 13, 14))
STEP = 256
NZ = 8


def fold(t):
    rows, n = t.shape
    t = t.reshape(rows // 16, 16, n)
    a = t[:, :8].reshape(rows // 2, n)
    b = t[:, 8:].reshape(rows // 2, n)
    r = lax.rem(lax.broadcasted_iota(jnp.int32, (rows // 2, 1), 0), 8)
    size = rows // 2
    low = jnp.where(r < 3, pltpu.roll(a, size - 5, 0), pltpu.roll(b, size - 2, 0))
    return jnp.where(r < CAP, a + b + low, 0.0)


def expand(h):
    rows, n = h.shape
    r = lax.rem(lax.broadcasted_iota(jnp.int32, (rows, 1), 0), 8)
    first = jnp.where(r < CAP, h, 0.0)
    third_a = jnp.where(r >= 5, pltpu.roll(h, 5, 0), 0.0)
    third_b = jnp.where((r == 5) | (r == 6), pltpu.roll(h, 2, 0), 0.0)
    none = jnp.zeros_like(first)

    def both(a, b):
        a, b = a.reshape(rows // 8, 8, n), b.reshape(rows // 8, 8, n)
        return jnp.concatenate([a, b], axis=1).reshape(rows * 2, n).astype(jnp.bfloat16)

    return both(first, none), both(none, first), both(third_a, third_b)


def pick(products):
    rows = products[0].shape[0]
    r = lax.rem(lax.broadcasted_iota(jnp.int32, (rows, 1), 0), 16)
    second = (r >= 8) & (r < 13)
    third = ((r >= 5) & (r < 8)) | (r >= 13)
    return jnp.where(second, products[1], jnp.where(third, products[2], products[0]))


def nt(a, b):
    return lax.dot_general(a, b, (((1,), (1,)), ((), ())), preferred_element_type=jnp.float32)


def nn(a, b):
    return jnp.dot(a, b, preferred_element_type=jnp.float32)


def stage_kernel(packed, stored, w_in, w_out, out, src, gat, win, wout, spx, preo_a, pret_a, preo_b, pret_b, obuf, xr,
                 own, zb, rz, fin, tb, lsem, wss, wrs, twss, twrs, gss, grs, xss, xrs, oss, ors, zss, zrs):
    me = lax.axis_index("ep")
    z = me // 4
    x = lax.rem(me // 2, 2)
    c = lax.rem(me, 2)
    other = 1 - c
    twin = z * 4 + x * 2 + other
    across = z * 4 + (1 - x) * 2 + c

    def at_z(zz):
        return zz * 4 + x * 2 + c

    def remote(a, b, ss, rs, device):
        return pltpu.make_async_remote_copy(
            src_ref=a, dst_ref=b, send_sem=ss, recv_sem=rs, device_id={"ep": device}, device_id_type=MESH)

    barrier = pltpu.get_barrier_semaphore()
    for device in [twin, across] + [at_z(lax.rem(z + d, NZ)) for d in range(1, NZ)]:
        pl.semaphore_signal(barrier, inc=1, device_id={"ep": device}, device_id_type=MESH)
    pl.semaphore_wait(barrier, 2 + NZ - 1)

    started = []
    pack_copies = []
    for s in range(2):
        copy = remote(packed.at[s, :, other], src.at[s, :, c], twss.at[s], twrs.at[s], twin)
        copy.start()
        pack_copies.append(copy)
        src[s, :, c] = packed[s, :, c]
    started += pack_copies

    weight_copies = []
    local_copies = []
    for p, (off, width) in enumerate(PARTS):
        mine = pl.multiple_of(c * HALF + off, 128)
        theirs = pl.multiple_of(other * HALF + off, 128)
        inner = pl.ds(p * LANES, width)
        down = pl.ds(pl.multiple_of(c * 128, 128), 128)
        pairs = (
            (w_in.at[pl.ds(mine, width)], w_in.at[pl.ds(theirs, width)], win.at[c, inner]),
            (w_out.at[:, pl.ds(mine, width)], w_out.at[:, pl.ds(theirs, width)], wout.at[down, inner]),
        )
        for k, (keep, give, slot) in enumerate(pairs):
            copy = remote(give, slot, wss.at[2 * p + k], wrs.at[2 * p + k], twin)
            copy.start()
            weight_copies.append(copy)
            copy = pltpu.make_async_copy(keep, slot, lsem.at[2 * p + k])
            copy.start()
            local_copies.append(copy)
        if width < LANES:
            win[:, p * LANES + width:(p + 1) * LANES] = jnp.zeros((2, LANES - width, 256), jnp.bfloat16)
            wout[:, p * LANES + width:(p + 1) * LANES] = jnp.zeros((256, LANES - width), jnp.bfloat16)
    copy = remote(stored, spx.at[c], wss.at[6], wrs.at[6], twin)
    copy.start()
    weight_copies.append(copy)
    spx[c] = stored[...]

    z_copies = [[], []]
    for s in range(2):
        pack_copies[s].wait_recv()
        for d in (1, 7, 2, 6, 3, 5, 4):
            to = lax.rem(z + d, NZ)
            copy = remote(src.at[s, to // 4], gat.at[s, x, z], gss.at[s, d], grs.at[s, d], at_z(to))
            copy.start()
            z_copies[s].append((d, copy))
        gat[s, x, z] = src[s, z // 4]

    x_copies = [[], []]

    def relay(s):
        copy = remote(gat.at[s, x, z], gat.at[s, x, z], xss.at[s, 0], xrs.at[s, 0], across)
        copy.start()
        x_copies[s].append(copy)
        for d, arriving in z_copies[s]:
            arriving.wait_recv()
            back = lax.rem(z + NZ - d, NZ)
            copy = remote(gat.at[s, x, back], gat.at[s, x, back], xss.at[s, d], xrs.at[s, d], across)
            copy.start()
            x_copies[s].append(copy)

    def pre(s, line):
        rows = gat[s, line].reshape(NZ * 32, LANES)
        if s == 0:
            for k in range(2):
                t = pick([nn(rows, win[k, p * LANES:(p + 1) * LANES]) for p in range(3)])
                preo_a[line, :, k * 256:(k + 1) * 256] = fold(t)
        else:
            t = pick([nt(rows, wout[:, p * LANES:(p + 1) * LANES]) for p in range(3)])
            preo_b[line] = fold(t)

    def swap_pre(s):
        mine, theirs = ((preo_a, pret_a), (preo_b, pret_b))[s]
        copy = remote(mine, theirs, twss.at[2 + s], twrs.at[2 + s], twin)
        copy.start()
        started.append(copy)
        return copy

    def hidden(s, line):
        if s == 0:
            g = preo_a[line] + pret_a[line]
            return jnp.concatenate([
                jax.nn.silu(g[:, 256 * k:256 * k + 128]) * g[:, 256 * k + 128:256 * k + 256] for k in range(2)], axis=1)
        g = preo_b[line] + pret_b[line]
        cols = []
        for k in range(2):
            ab = spx[k, line].astype(jnp.float32)
            a, b = ab[:, :128], ab[:, 128:]
            q = jax.nn.sigmoid(a)
            gk = g[:, 128 * k:128 * k + 128]
            cols += [gk * b * q * (1.0 + a * (1.0 - q)), gk * a * q]
        return jnp.concatenate(cols, axis=1)

    def post(s, line, emit):
        parts = expand(hidden(s, line))

        @pl.loop(0, LANES // STEP)
        def _(n):
            total = None
            for p in range(3):
                cols = pl.ds(pl.multiple_of(p * LANES + n * STEP, STEP), STEP)
                if s == 0:
                    terms = [nn(parts[p], wout[:, cols])]
                else:
                    terms = [nt(parts[p][:, 256 * k:256 * k + 256], win[k, cols]) for k in range(2)]
                for term in terms:
                    total = term if total is None else total + term
            emit(n, total)

    def chunk(s, n):
        cols = pl.ds(pl.multiple_of(n * STEP, STEP), STEP)
        return remote(obuf.at[s, :, cols], xr.at[s, :, cols], oss.at[s, n], ors.at[s, n], across)

    def give_across(s):
        def emit(n, total):
            obuf[s, :, pl.ds(pl.multiple_of(n * STEP, STEP), STEP)] = total.astype(jnp.bfloat16)
            chunk(s, n).start()

        post(s, 1 - x, emit)

    def keep(s):
        def emit(n, total):
            own[s, :, pl.ds(pl.multiple_of(n * STEP, STEP), STEP)] = total

        post(s, x, emit)

    back_copies = [[], []]

    def give_back(s):
        @pl.loop(0, LANES // STEP)
        def _(n):
            cols = pl.ds(pl.multiple_of(n * STEP, STEP), STEP)
            chunk(s, n).wait_recv()
            total = own[s, :, cols] + xr[s, :, cols].astype(jnp.float32)
            zb[s, :, :, :, cols] = total.astype(jnp.bfloat16).reshape(NZ, 2, 16, STEP)

        for d in (4, 3, 5, 2, 6, 1, 7):
            to = lax.rem(z + d, NZ)
            copy = remote(zb.at[s, to], rz.at[s, z], zss.at[s, d], zrs.at[s, d], at_z(to))
            copy.start()
            back_copies[s].append(copy)
        rz[s, z] = zb[s, z]

    def finish(s):
        for copy in back_copies[s]:
            copy.wait_recv()
        for e in range(2):
            for core, slot in ((c, out.at[s, e, c]), (other, tb.at[s, e])):
                total = rz[s, 4 * e, core].astype(jnp.float32)
                for i in range(1, 4):
                    total = total + rz[s, 4 * e + i, core].astype(jnp.float32)
                slot[...] = total
        copy = remote(tb.at[s], fin.at[s], twss.at[4 + s], twrs.at[4 + s], twin)
        copy.start()
        started.append(copy)
        return copy

    def arrived(s):
        for copy in x_copies[s]:
            copy.wait_recv()

    relay(0)
    for copy in local_copies:
        copy.wait()
    for copy in weight_copies:
        copy.wait_recv()
    pre(0, x)
    relay(1)
    arrived(0)
    pre(0, 1 - x)
    swap_a = swap_pre(0)
    pre(1, x)
    swap_a.wait_recv()
    give_across(0)
    keep(0)
    arrived(1)
    pre(1, 1 - x)
    swap_b = swap_pre(1)
    give_back(0)
    swap_b.wait_recv()
    give_across(1)
    keep(1)
    give_back(1)
    last = [finish(0), finish(1)]
    for s in range(2):
        last[s].wait_recv()
        out[s, :, other] = fin[s]

    for copy in started + weight_copies:
        copy.wait_send()
    for s in range(2):
        for _, copy in z_copies[s]:
            copy.wait_send()
        for copy in x_copies[s] + back_copies[s]:
            copy.wait_send()

        @pl.loop(0, LANES // STEP)
        def _(n):
            chunk(s, n).wait_send()


def run_stage(packed, stored, w_in, w_out):
    bf16, f32 = jnp.bfloat16, jnp.float32
    vmem = pl.BlockSpec(memory_space=pltpu.VMEM)
    hbm = pl.BlockSpec(memory_space=pl.ANY)
    dma = pltpu.SemaphoreType.DMA
    return pl.pallas_call(
        stage_kernel,
        out_shape=jax.ShapeDtypeStruct((2, 2, 2, 16, LANES), f32),
        in_specs=[vmem, vmem, hbm, hbm],
        out_specs=vmem,
        scratch_shapes=[
            pltpu.VMEM((2, 2, 2, 16, LANES), bf16),
            pltpu.VMEM((2, 2, NZ, 2, 16, LANES), bf16),
            pltpu.VMEM((2, 3 * LANES, 256), bf16),
            pltpu.VMEM((256, 3 * LANES), bf16),
            pltpu.VMEM((2, 2, 128, 256), bf16),
            pltpu.VMEM((2, 128, 512), f32),
            pltpu.VMEM((2, 128, 512), f32),
            pltpu.VMEM((2, 128, 256), f32),
            pltpu.VMEM((2, 128, 256), f32),
            pltpu.VMEM((2, 256, LANES), bf16),
            pltpu.VMEM((2, 256, LANES), bf16),
            pltpu.VMEM((2, 256, LANES), f32),
            pltpu.VMEM((2, NZ, 2, 16, LANES), bf16),
            pltpu.VMEM((2, NZ, 2, 16, LANES), bf16),
            pltpu.VMEM((2, 2, 16, LANES), f32),
            pltpu.VMEM((2, 2, 16, LANES), f32),
            dma((6,)),
            dma((7,)), dma((7,)),
            dma((6,)), dma((6,)),
            dma((2, 8)), dma((2, 8)),
            dma((2, 8)), dma((2, 8)),
            dma((2, 5)), dma((2, 5)),
            dma((2, 8)), dma((2, 8)),
        ],
        compiler_params=pltpu.CompilerParams(
            collective_id=0, has_side_effects=True, vmem_limit_bytes=48 * 2 ** 20),
        name="expert_stage",
    )(packed, stored, w_in, w_out)


def passed_along(value, axis, steps):
    count = lax.axis_size(axis)
    pairs = [(source, (source + steps) % count) for source in range(count)]
    return lax.ppermute(value, axis, pairs)


def slot_tables(expert_ids, weights):
    labels = jnp.arange(EXP_SEC, dtype=jnp.int32)
    is_named = expert_ids[:, :, None] == labels[None, None, :]
    member = jnp.any(is_named, axis=1)
    scales = jnp.sum(jnp.where(is_named, weights[:, :, None], 0.0), axis=1)
    slot_rank = jnp.cumsum(member.astype(jnp.int32), axis=0) - 1
    places = jnp.arange(CAP, dtype=jnp.int32)
    onehot = member[:, :, None] & (slot_rank[:, :, None] == places[None, None, :])
    choose = jnp.transpose(onehot, (1, 2, 0)).reshape(EXP_SEC * CAP, -1)
    scaled = jnp.transpose(onehot * scales[:, :, None], (1, 2, 0)).reshape(EXP_SEC * CAP, -1)
    return choose.astype(jnp.float32), scaled


def to_tiles(rows):
    rows = rows.reshape(EXP_SEC, CAP, 2, HALF)
    pieces = [jnp.pad(rows[..., off:off + w], ((0, 0), (0, 0), (0, 0), (0, LANES - w))) for off, w in PARTS]
    pieces = [jnp.transpose(p, (0, 2, 1, 3)) for p in pieces]
    blank = jnp.zeros_like(pieces[0][:, :, :1])
    return jnp.concatenate([pieces[0], pieces[2][:, :, :3], pieces[1], pieces[2][:, :, 3:], blank], axis=2)


def from_tiles(tiles):
    pieces = [tiles[:, :, 0:5], tiles[:, :, 8:13], jnp.concatenate([tiles[:, :, 5:8], tiles[:, :, 13:15]], axis=2)]
    rows = jnp.concatenate([p[..., :w] for p, (_, w) in zip(pieces, PARTS)], axis=3)
    return jnp.transpose(rows, (0, 2, 1, 3)).reshape(EXP_SEC * CAP, 2 * HALF)


def choose_rows(choose, tokens):
    return jnp.dot(choose.astype(jnp.bfloat16), tokens, preferred_element_type=jnp.float32).astype(jnp.bfloat16)


def updated(rows, choose, scaled, tiles):
    mix = lax.dot_general(choose, scaled, (((1,), (1,)), ((), ())), precision=lax.Precision.HIGHEST)
    added = jnp.dot(mix, from_tiles(tiles), precision=lax.Precision.HIGHEST)
    return (rows.astype(jnp.float32) + added).astype(jnp.bfloat16)


def place(choose, rows, tokens):
    first = jnp.cumsum(choose, axis=0)
    lone = jnp.where(first == 1.0, choose, 0.0).astype(jnp.bfloat16)
    put = lax.dot_general(lone, rows, (((0,), (0,)), ((), ())), preferred_element_type=jnp.float32)
    touched = jnp.sum(choose, axis=0) > 0.0
    return jnp.where(touched[:, None], put.astype(jnp.bfloat16), tokens)


def local(forward_in, grad_in, routes, gate_weights, saved_preact, gate_up, down_proj):
    w_in = gate_up[0, 0]
    w_out = down_proj[0, 0]
    starts = (forward_in[0], grad_in[0])
    steps = (1, -1)
    tables = [[slot_tables(routes[0, t, s], gate_weights[0, t, s]) for s in range(2)] for t in range(2)]
    stored = jnp.transpose(saved_preact[0, :, 0].reshape(2, NZ, 2, 2, CAP, 256), (0, 2, 1, 3, 4, 5))
    stored = jnp.pad(stored, ((0, 0), (0, 0), (0, 0), (0, 0), (0, 8 - CAP), (0, 0))).reshape(2, 2, 128, 256)

    bulk = [passed_along(starts[s], "pp", 2 * steps[s]) for s in range(2)]
    rows = []
    for s in range(2):
        ahead = passed_along(tables[0][s][0].astype(jnp.bfloat16), "pp", -steps[s])
        rows.append(passed_along(choose_rows(ahead, starts[s]), "pp", steps[s]))
    sums = run_stage(jnp.stack([to_tiles(r) for r in rows]), stored[0], w_in, w_out)
    mids = []
    for s in range(2):
        choose, scaled = tables[0][s]
        fresh = passed_along(updated(rows[s], choose, scaled, sums[s]), "pp", steps[s])
        chosen = passed_along(choose.astype(jnp.bfloat16), "pp", steps[s])
        mids.append(place(chosen.astype(jnp.float32), fresh, bulk[s]))
    rows = [choose_rows(tables[1][s][0], mids[s]) for s in range(2)]
    sums = run_stage(jnp.stack([to_tiles(r) for r in rows]), stored[1], w_in, w_out)
    outs = []
    for s in range(2):
        choose, scaled = tables[1][s]
        outs.append(place(choose, updated(rows[s], choose, scaled, sums[s]), mids[s]))
    return (outs[0][None], outs[1][None])


def solution(mesh):
    in_specs = (
        P("pp", "ep", None),
        P("pp", "ep", None),
        P("pp", None, None, "ep", None),
        P("pp", None, None, "ep", None),
        P("pp", None, "ep", None, None, None),
        P("pp", "ep", None, None),
        P("pp", "ep", None, None),
    )
    out_specs = (P("pp", "ep", None), P("pp", "ep", None))
    return jax.shard_map(local, mesh=mesh, in_specs=in_specs, out_specs=out_specs, check_vma=False)
```

time: 814 us -> 248 us (0.30)
  waiting for transfers between devices: 636 us -> 9.88 us
  Pallas kernels: 0 us -> 183 us
  local copies, waits for them, and re-layouts: 47.9 us -> 9.19 us
  starting transfers between devices: 63.6 us -> 26.9 us
  matrix products: 51.4 us -> 15 us
  other arithmetic: 12.3 us -> 1.52 us
    all_to_all x8 -> x0, waiting for transfers between devices: 368 us -> none  [the longest x4 227 us: return_sums(): lax.all_to_all(partial_value, 'ep', split_axis=0, concat_axis=0, tiled=True)]
    ppermute x4 -> x10, waiting for transfers between devices: 268 us -> 9.88 us  [passed_along(): return lax.ppermute(value, axis, pairs)]
    pallas_call x0 -> x2, Pallas kernels: none -> 183 us  [run_stage(): pl.pallas_call(stage_kernel, out_shape=jax.ShapeDtypeStruct((2, 2, 2, 16,...]
    all_to_all x8 -> x0, starting transfers between devices: 51.8 us -> none  [the longest x4 32.3 us: send_rows(): lax.all_to_all(outgoing, 'ep', split_axis=0, concat_axis=0, tiled=True)]
    dot_general x16, matrix products: 51.4 us -> 15 us  [the longest x4 8.1 us: place(): lax.dot_general(lone, rows, (((0,), (0,)), ((), ())), preferred_element_t...]
    reshape x8 -> x4, local copies, waits for them, and re-layouts: 36.7 us -> 0.38 us  [to_tiles(): rows = rows.reshape(EXP_SEC, CAP, 2, HALF)]
    ppermute x4 -> x10, starting transfers between devices: 11.7 us -> 26.9 us  [passed_along(): return lax.ppermute(value, axis, pairs)]
    reduce_sum x7 -> x4, other arithmetic: 11.5 us -> 0.08 us  [the longest x2 0.04 us: slot_tables(): scales = jnp.sum(jnp.where(is_named, weights[:, :, None], 0.0), axis=1)]
  transfers between devices with their start and end apart: 12 -> 10, of which waited for: 10 -> 3; matrix products, arithmetic and copies ran while one was open for 11% -> 4% of each run, Pallas kernels for 0% -> 38%
where the time goes in v1:
time: 248 us
  Pallas kernels  183 us (74%)
  starting transfers between devices  26.9 us (11%)
  matrix products  15 us (6%)
  waiting for transfers between devices  9.88 us (4%)
  local copies, waits for them, and re-layouts  9.19 us (4%)
    pallas_call x2, Pallas kernels, run_stage(): pl.pallas_call(stage_kernel, out_shape=jax.ShapeDtypeStruct((2, 2, 2, 16,...  183 us
    ppermute x10, starting transfers between devices, passed_along(): return lax.ppermute(value, axis, pairs)  26.9 us
    ppermute x10, waiting for transfers between devices, passed_along(): return lax.ppermute(value, axis, pairs)  9.88 us
    dot_general x4, matrix products, place(): lax.dot_general(lone, rows, (((0,), (0,)), ((), ())), preferred_element_t...  8.1 us
  transfers between devices with their start and end apart: 10, of which 3 were waited for; matrix products, arithmetic and copies ran while one was open for 4% of the time, Pallas kernels for 38%

profile of v1, /device:TPU:1, one launch (start us, length us, event | category | flops | bytes accessed | tf_op | source)
XLA Modules:
  0.0 247.7 jit_solution(15226956739071239725)
XLA Ops:
  0.7 0.8 slice_bitcast_fusion.6
  3.3 3.6 %collective-permute-start = (bf16[10,128]{1,0:T(8,128)(2,1)S(1)}, bf16[10,128]{1,0:T(8,128)(2,1)S(1)}, u32[]{:S(2)}, u32[]{:S(2)}) collective-permute-start(bf16[10,128]{1,0:T(8,128)(2,1)S(1)} %get-tuple-element.29), channel_id=1, source_target_pairs={{0,32},{32,64},{64,96},{96,128},{128,160},{160,192},{192,224},{224... | collective-permute-start | bytes 7688 | tf_op jit(solution)/shard_map/ppermute | solution.py:329
  6.9 2.5 %collective-permute-start.1 = (bf16[10,128]{1,0:T(8,128)(2,1)S(1)}, bf16[10,128]{1,0:T(8,128)(2,1)S(1)}, u32[]{:S(2)}, u32[]{:S(2)}) collective-permute-start(bf16[10,128]{1,0:T(8,128)(2,1)S(1)} %get-tuple-element.29), channel_id=1, source_target_pairs={{0,224},{32,0},{64,32},{96,64},{128,96},{160,128},{192,160},{224,1... | collective-permute-start | bytes 7688 | tf_op jit(solution)/shard_map/ppermute | solution.py:329
  9.9 4.7 %collective-permute-start.7 = (bf16[10,128]{1,0:T(8,128)(2,1)S(1)}, bf16[10,128]{1,0:T(8,128)(2,1)S(1)}, u32[]{:S(2)}, u32[]{:S(2)}) collective-permute-start(bf16[10,128]{1,0:T(8,128)(2,1)S(1)} %get-tuple-element.30), channel_id=1, source_target_pairs={{0,224},{32,0},{64,32},{96,64},{128,96},{160,128},{192,160},{224,1... | collective-permute-start | bytes 7688 | tf_op jit(solution)/shard_map/ppermute | solution.py:329
  15.7 2.7 %collective-permute-start.9 = (bf16[128,7168]{1,0:T(8,128)(2,1)}, bf16[128,7168]{1,0:T(8,128)(2,1)}, u32[]{:S(2)}, u32[]{:S(2)}) collective-permute-start(bf16[128,7168]{1,0:T(8,128)(2,1)} %bitcast.16), channel_id=1, source_target_pairs={{0,192},{32,224},{64,0},{96,32},{128,64},{160,96},{192,128},{224,1... | collective-permute-start | bytes 5505032 | tf_op jit(solution)/shard_map/ppermute | solution.py:329
  18.4 1.8 convolution_convert_fusion.7
  20.4 1.8 convolution_convert_fusion.6
  22.3 5.3 %collective-permute-start.4 = (bf16[10,7168]{1,0:T(8,128)(2,1)S(1)}, bf16[10,7168]{1,0:T(8,128)(2,1)S(1)}, u32[]{:S(2)}, u32[]{:S(2)}) collective-permute-start(bf16[10,7168]{1,0:T(8,128)(2,1)S(1)} %convolution_convert_fusion.6), channel_id=1, source_target_pairs={{0,224},{32,0},{64,32},{96,64},{128,96},{160,128},{192,160},{224,1... | collective-permute-start | bytes 430088 | tf_op jit(solution)/shard_map/ppermute | solution.py:329
  27.7 3.6 %collective-permute-done.4 = bf16[10,7168]{1,0:T(8,128)(2,1)S(1)} collective-permute-done((bf16[10,7168]{1,0:T(8,128)(2,1)S(1)}, bf16[10,7168]{1,0:T(8,128)(2,1)S(1)}, u32[]{:S(2)}, u32[]{:S(2)}) %collective-permute-start.4) | collective-permute-done | bytes 143392 | tf_op jit(solution)/shard_map/ppermute | solution.py:329
  32.4 0.6 copy-done
  33.0 94.2 %expert_stage.2 = f32[2,2,2,16,1280]{4,3,2,1,0:T(8,128)S(1)} custom-call(bf16[2,2,2,16,1280]{4,3,2,1,0:T(8,128)(2,1)S(1)} %pad_maximum_fusion.4.packed, bf16[2,128,256]{2,1,0:T(8,128)(2,1)S(1)} %bitcast.142, bf16[7168,256]{1,0:T(8,128)(2,1)} %bitcast.143, bf16[128,7168]{1,0:T(8,128)(2,1)S(1)} %bitcast.139), custom_call_target="tpu_custom_call" | custom-call | tf_op jit(solution)/shard_map/expert_stage/pallas_call | solution.py:290
  128.6 0.5 add_convert_fusion.2
  129.1 7.3 %collective-permute-start.8 = (bf16[10,7168]{1,0:T(8,128)(2,1)S(1)}, bf16[10,7168]{1,0:T(8,128)(2,1)S(1)}, u32[]{:S(2)}, u32[]{:S(2)}) collective-permute-start(bf16[10,7168]{1,0:T(8,128)(2,1)S(1)} %add_convert_fusion.2), channel_id=1, source_target_pairs={{0,224},{32,0},{64,32},{96,64},{128,96},{160,128},{192,160},{224,1... | collective-permute-start | bytes 430088 | tf_op jit(solution)/shard_map/ppermute | solution.py:329
  136.3 0.5 add_convert_fusion.3
  137.2 4.0 %collective-permute-done.8 = bf16[10,7168]{1,0:T(8,128)(2,1)S(1)} collective-permute-done((bf16[10,7168]{1,0:T(8,128)(2,1)S(1)}, bf16[10,7168]{1,0:T(8,128)(2,1)S(1)}, u32[]{:S(2)}, u32[]{:S(2)}) %collective-permute-start.8) | collective-permute-done | bytes 143392 | tf_op jit(solution)/shard_map/ppermute | solution.py:329
  141.2 2.2 broadcast_select_fusion
  143.4 1.2 copy-done.1
  145.3 2.2 collective-permute-done.5
  147.5 2.2 broadcast_select_fusion.1
  149.7 1.2 copy-done.3
  152.0 89.3 %expert_stage.3 = f32[2,2,2,16,1280]{4,3,2,1,0:T(8,128)S(1)} custom-call(bf16[2,2,2,16,1280]{4,3,2,1,0:T(8,128)(2,1)S(1)} %pad_maximum_fusion.5.packed, bf16[2,128,256]{2,1,0:T(8,128)(2,1)S(1)} %bitcast.141, bf16[7168,256]{1,0:T(8,128)(2,1)} %bitcast.144, bf16[128,7168]{1,0:T(8,128)(2,1)S(1)} %bitcast.140), custom_call_target="tpu_custom_call" | custom-call | tf_op jit(solution)/shard_map/expert_stage/pallas_call | solution.py:290
  242.6 0.5 fusion.49
  243.9 1.9 fusion.1
  245.8 1.9 fusion.3
  (183 shorter events, 9.4 us)
Async XLA Ops:
  0.6 14.0 %copy-start.6 = (f32[1,2,2,128,8]{3,4,2,1,0:T(8,128)S(1)}, f32[1,2,2,128,8]{3,4,2,1,0:T(8,128)}, u32[]{:S(2)}) copy-start(f32[1,2,2,128,8]{3,4,2,1,0:T(8,128)} %param.10) | copy-start | bytes 49156
  0.6 14.0 %copy-start.5 = (bf16[1,2,1,32,5,256]{5,3,4,2,1,0:T(8,128)(2,1)S(1)}, bf16[1,2,1,32,5,256]{5,3,4,2,1,0:T(8,128)(2,1)}, u32[]{:S(2)}) copy-start(bf16[1,2,1,32,5,256]{5,3,4,2,1,0:T(8,128)(2,1)} %param.11) | copy-start | bytes 491524
  3.3 12.4 %collective-permute-start = (bf16[10,128]{1,0:T(8,128)(2,1)S(1)}, bf16[10,128]{1,0:T(8,128)(2,1)S(1)}, u32[]{:S(2)}, u32[]{:S(2)}) collective-permute-start(bf16[10,128]{1,0:T(8,128)(2,1)S(1)} %get-tuple-element.29), channel_id=1, source_target_pairs={{0,32},{32,64},{64,96},{96,128},{128,160},{160,192},{192,224},{224... | collective-permute-start | bytes 7688 | tf_op jit(solution)/shard_map/ppermute | solution.py:329
  6.9 11.5 %collective-permute-start.1 = (bf16[10,128]{1,0:T(8,128)(2,1)S(1)}, bf16[10,128]{1,0:T(8,128)(2,1)S(1)}, u32[]{:S(2)}, u32[]{:S(2)}) collective-permute-start(bf16[10,128]{1,0:T(8,128)(2,1)S(1)} %get-tuple-element.29), channel_id=1, source_target_pairs={{0,224},{32,0},{64,32},{96,64},{128,96},{160,128},{192,160},{224,1... | collective-permute-start | bytes 7688 | tf_op jit(solution)/shard_map/ppermute | solution.py:329
  9.5 10.9 %collective-permute-start.3 = (bf16[10,128]{1,0:T(8,128)(2,1)S(1)}, bf16[10,128]{1,0:T(8,128)(2,1)S(1)}, u32[]{:S(2)}, u32[]{:S(2)}) collective-permute-start(bf16[10,128]{1,0:T(8,128)(2,1)S(1)} %get-tuple-element.30), channel_id=1, source_target_pairs={{0,32},{32,64},{64,96},{96,128},{128,160},{160,192},{192,224},{224... | collective-permute-start | bytes 7688 | tf_op jit(solution)/shard_map/ppermute | solution.py:329
  9.9 17.7 %collective-permute-start.7 = (bf16[10,128]{1,0:T(8,128)(2,1)S(1)}, bf16[10,128]{1,0:T(8,128)(2,1)S(1)}, u32[]{:S(2)}, u32[]{:S(2)}) collective-permute-start(bf16[10,128]{1,0:T(8,128)(2,1)S(1)} %get-tuple-element.30), channel_id=1, source_target_pairs={{0,224},{32,0},{64,32},{96,64},{128,96},{160,128},{192,160},{224,1... | collective-permute-start | bytes 7688 | tf_op jit(solution)/shard_map/ppermute | solution.py:329
  14.5 133.0 %collective-permute-start.6 = (bf16[128,7168]{1,0:T(8,128)(2,1)}, bf16[128,7168]{1,0:T(8,128)(2,1)}, u32[]{:S(2)}, u32[]{:S(2)}) collective-permute-start(bf16[128,7168]{1,0:T(8,128)(2,1)} %bitcast.6), channel_id=1, source_target_pairs={{0,64},{32,96},{64,128},{96,160},{128,192},{160,224},{192,0},{224,... | collective-permute-start | bytes 5505032 | tf_op jit(solution)/shard_map/ppermute | solution.py:329
  15.7 125.5 %collective-permute-start.9 = (bf16[128,7168]{1,0:T(8,128)(2,1)}, bf16[128,7168]{1,0:T(8,128)(2,1)}, u32[]{:S(2)}, u32[]{:S(2)}) collective-permute-start(bf16[128,7168]{1,0:T(8,128)(2,1)} %bitcast.16), channel_id=1, source_target_pairs={{0,192},{32,224},{64,0},{96,32},{128,64},{160,96},{192,128},{224,1... | collective-permute-start | bytes 5505032 | tf_op jit(solution)/shard_map/ppermute | solution.py:329
  20.3 11.3 %collective-permute-start.2 = (bf16[10,7168]{1,0:T(8,128)(2,1)S(1)}, bf16[10,7168]{1,0:T(8,128)(2,1)S(1)}, u32[]{:S(2)}, u32[]{:S(2)}) collective-permute-start(bf16[10,7168]{1,0:T(8,128)(2,1)S(1)} %convolution_convert_fusion.7), channel_id=1, source_target_pairs={{0,32},{32,64},{64,96},{96,128},{128,160},{160,192},{192,224},{224... | collective-permute-start | bytes 430088 | tf_op jit(solution)/shard_map/ppermute | solution.py:329
  22.3 9.0 %collective-permute-start.4 = (bf16[10,7168]{1,0:T(8,128)(2,1)S(1)}, bf16[10,7168]{1,0:T(8,128)(2,1)S(1)}, u32[]{:S(2)}, u32[]{:S(2)}) collective-permute-start(bf16[10,7168]{1,0:T(8,128)(2,1)S(1)} %convolution_convert_fusion.6), channel_id=1, source_target_pairs={{0,224},{32,0},{64,32},{96,64},{128,96},{160,128},{192,160},{224,1... | collective-permute-start | bytes 430088 | tf_op jit(solution)/shard_map/ppermute | solution.py:329
  31.5 1.5 copy-start
  129.1 12.1 %collective-permute-start.8 = (bf16[10,7168]{1,0:T(8,128)(2,1)S(1)}, bf16[10,7168]{1,0:T(8,128)(2,1)S(1)}, u32[]{:S(2)}, u32[]{:S(2)}) collective-permute-start(bf16[10,7168]{1,0:T(8,128)(2,1)S(1)} %add_convert_fusion.2), channel_id=1, source_target_pairs={{0,224},{32,0},{64,32},{96,64},{128,96},{160,128},{192,160},{224,1... | collective-permute-start | bytes 430088 | tf_op jit(solution)/shard_map/ppermute | solution.py:329
  136.9 10.7 %collective-permute-start.5 = (bf16[10,7168]{1,0:T(8,128)(2,1)S(1)}, bf16[10,7168]{1,0:T(8,128)(2,1)S(1)}, u32[]{:S(2)}, u32[]{:S(2)}) collective-permute-start(bf16[10,7168]{1,0:T(8,128)(2,1)S(1)} %add_convert_fusion.3), channel_id=1, source_target_pairs={{0,32},{32,64},{64,96},{96,128},{128,160},{160,192},{192,224},{224... | collective-permute-start | bytes 430088 | tf_op jit(solution)/shard_map/ppermute | solution.py:329
  143.4 1.2 copy-start.1
  149.7 1.2 copy-start.3
  242.4 1.5 copy-start.4
  243.9 1.9 copy-start.2

commit v2 on v0

v2 whole, which is shorter than its diff:
```python
import functools

import jax
import jax.numpy as jnp
from jax import lax
from jax.experimental import pallas as pl
from jax.experimental.pallas import tpu as pltpu
from jax.sharding import PartitionSpec as P

EXP_SEC = 2
SEGMENTS = 2
CAP = 5
MESH = pl.DeviceIdType.MESH

HALF = 3584
LANES = 1280
PARTS = ((0, 1280), (1280, 1152), (2432, 1152))
PART_ROWS = ((0, 1, 2, 3, 4), (8, 9, 10, 11, 12), (5, 6, 7, 13, 14))
STEP = 256
NZ = 8


def fold(t):
    rows, n = t.shape
    t = t.reshape(rows // 16, 16, n)
    a = t[:, :8].reshape(rows // 2, n)
    b = t[:, 8:].reshape(rows // 2, n)
    r = lax.rem(lax.broadcasted_iota(jnp.int32, (rows // 2, 1), 0), 8)
    size = rows // 2
    low = jnp.where(r < 3, pltpu.roll(a, size - 5, 0), pltpu.roll(b, size - 2, 0))
    return jnp.where(r < CAP, a + b + low, 0.0)


def expand(h, dtype=jnp.bfloat16):
    rows, n = h.shape
    r = lax.rem(lax.broadcasted_iota(jnp.int32, (rows, 1), 0), 8)
    first = jnp.where(r < CAP, h, 0.0)
    third_a = jnp.where(r >= 5, pltpu.roll(h, 5, 0), 0.0)
    third_b = jnp.where((r == 5) | (r == 6), pltpu.roll(h, 2, 0), 0.0)
    none = jnp.zeros_like(first)

    def both(a, b):
        a, b = a.reshape(rows // 8, 8, n), b.reshape(rows // 8, 8, n)
        return jnp.concatenate([a, b], axis=1).reshape(rows * 2, n).astype(dtype)

    return both(first, none), both(none, first), both(third_a, third_b)


def pick(products):
    rows = products[0].shape[0]
    r = lax.rem(lax.broadcasted_iota(jnp.int32, (rows, 1), 0), 16)
    second = (r >= 8) & (r < 13)
    third = ((r >= 5) & (r < 8)) | (r >= 13)
    return jnp.where(second, products[1], jnp.where(third, products[2], products[0]))


def nt(a, b):
    return lax.dot_general(a, b, (((1,), (1,)), ((), ())), preferred_element_type=jnp.float32)


def tn(a, b):
    return lax.dot_general(a, b, (((0,), (0,)), ((), ())), preferred_element_type=jnp.float32)


def nn(a, b):
    return jnp.dot(a, b, preferred_element_type=jnp.float32)


def tables(ids, weights=None):
    tokens = ids.shape[1]
    before = lax.broadcasted_iota(jnp.int32, (tokens, tokens), 0) <= lax.broadcasted_iota(jnp.int32, (tokens, tokens), 1)
    before = before.astype(jnp.float32).astype(jnp.bfloat16)
    place = lax.broadcasted_iota(jnp.int32, (8, tokens), 0).astype(jnp.float32)
    choose, scaled, lone, member = [], [], [], []
    for e in range(EXP_SEC):
        hit = ids == e
        named = jnp.sum(hit.astype(jnp.float32), axis=0, keepdims=True) + jnp.zeros((8, tokens), jnp.float32)
        rank = nn(named.astype(jnp.bfloat16), before)
        slot = jnp.where((named > 0.0) & (rank - 1.0 == place) & (place < CAP), 1.0, 0.0)
        choose.append(slot)
        lone.append(slot if e == 0 else slot * (1.0 - member[0]))
        member.append(named)
        if weights is not None:
            scaled.append(slot * jnp.sum(jnp.where(hit, weights, 0.0), axis=0, keepdims=True))
    choose, lone = jnp.concatenate(choose, axis=0), jnp.concatenate(lone, axis=0)
    scaled = jnp.concatenate(scaled, axis=0) if weights is not None else None
    touched = jnp.maximum(member[0], member[1])
    return choose, scaled, lone, touched


def pack(parts, tokens, half):
    wide = None
    for p, (off, width) in enumerate(PARTS):
        got = nn(parts[p], tokens[:, half * HALF + off:half * HALF + off + width])
        if width < LANES:
            got = jnp.concatenate([got, jnp.zeros((got.shape[0], LANES - width), jnp.float32)], axis=1)
        wide = got if wide is None else wide + got
    return wide


def relay_kernel(x_in, y_in, ids, weights, stored, w_in, w_out, out, xv, xb, rt0, rt2, idt, wtt, pk, src, gat, win, wout,
                 spx, preo_a, pret_a, preo_b, pret_b, obuf, xr, own, zb, rz, mt, nv, nw, base, lsem, wss, wrs, tss, trs,
                 pss, prs, bss, brs, twss, twrs, gss, grs, xss, xrs, oss, ors, zss, zrs):
    me = lax.axis_index("ep")
    pp = lax.axis_index("pp")
    n_pp = lax.axis_size("pp")
    z = me // 4
    x = lax.rem(me // 2, 2)
    c = lax.rem(me, 2)
    other = 1 - c
    twin = z * 4 + x * 2 + other
    across = z * 4 + (1 - x) * 2 + c
    steps = (1, n_pp - 1)
    bf16, f32 = jnp.bfloat16, jnp.float32

    def at_z(zz):
        return zz * 4 + x * 2 + c

    def remote(a, b, ss, rs, device, section=None):
        where = {"ep": device} if section is None else {"pp": section, "ep": device}
        return pltpu.make_async_remote_copy(
            src_ref=a, dst_ref=b, send_sem=ss, recv_sem=rs, device_id=where, device_id_type=MESH)

    def section(hops):
        return lax.rem(pp + hops, n_pp)

    partners = [{"ep": twin}, {"ep": across}] + [{"ep": at_z(lax.rem(z + d, NZ))} for d in range(1, NZ)]
    for hops in (1, n_pp - 1):
        partners += [{"pp": section(hops), "ep": me}, {"pp": section(hops), "ep": twin}]
    for hops in (2, n_pp - 2):
        partners.append({"pp": section(hops), "ep": me})
    locals_x = []
    for s, tokens in enumerate((x_in, y_in)):
        copy = pltpu.make_async_copy(tokens, xv.at[s], lsem.at[6 + s])
        copy.start()
        locals_x.append(copy)
    barrier = pltpu.get_barrier_semaphore()
    for device in partners:
        pl.semaphore_signal(barrier, inc=1, device_id=device, device_id_type=MESH)
    pl.semaphore_wait(barrier, len(partners))

    started = []

    def go(copy):
        copy.start()
        started.append(copy)
        return copy

    ahead, behind = [], []
    for s in range(2):
        ahead.append(go(remote(ids.at[0, s], rt0.at[s], tss.at[s, 0], trs.at[s, 0], me, section(n_pp - steps[s]))))
    for s in range(2):
        behind.append(go(remote(ids.at[0, s], rt2.at[s], tss.at[s, 1], trs.at[s, 1], me, section(steps[s]))))
    twin_tables = [go(remote(ids, idt, twss.at[0], twrs.at[0], twin)),
                   go(remote(weights, wtt, twss.at[1], twrs.at[1], twin))]

    weight_copies, local_copies = [], []
    for p, (off, width) in enumerate(PARTS):
        mine = pl.multiple_of(c * HALF + off, 128)
        theirs = pl.multiple_of(other * HALF + off, 128)
        inner = pl.ds(p * LANES, width)
        down = pl.ds(pl.multiple_of(c * 128, 128), 128)
        pairs = (
            (w_in.at[pl.ds(mine, width)], w_in.at[pl.ds(theirs, width)], win.at[c, inner]),
            (w_out.at[:, pl.ds(mine, width)], w_out.at[:, pl.ds(theirs, width)], wout.at[down, inner]),
        )
        for k, (keep_part, give_part, slot) in enumerate(pairs):
            weight_copies.append(go(remote(give_part, slot, wss.at[2 * p + k], wrs.at[2 * p + k], twin)))
            copy = pltpu.make_async_copy(keep_part, slot, lsem.at[2 * p + k])
            copy.start()
            local_copies.append(copy)
        if width < LANES:
            win[:, p * LANES + width:(p + 1) * LANES] = jnp.zeros((2, LANES - width, 256), bf16)
            wout[:, p * LANES + width:(p + 1) * LANES] = jnp.zeros((256, LANES - width), bf16)
    weight_copies.append(go(remote(stored, spx.at[c], wss.at[6], wrs.at[6], twin)))
    spx[c] = stored[...]

    first_rows = []
    for s in range(2):
        ahead[s].wait_recv()
        locals_x[s].wait()
        parts = expand(tables(rt0[s])[0])
        for half in range(2):
            pk[0, s, half] = pack(parts, xv.at[s], half).astype(bf16).reshape(2, 16, LANES)
        first_rows.append([
            go(remote(pk.at[0, s, half], src.at[0, s, :, c], pss.at[0, s, i], prs.at[0, s, i],
                      (me, twin)[i], section(steps[s])))
            for i, half in enumerate((c, other))])

    bulk = [go(remote(tokens, xb.at[s], bss.at[s], brs.at[s], me, section(2 * steps[s] if s == 0 else n_pp - 2)))
            for s, tokens in enumerate((x_in, y_in))]

    z_copies, x_copies, back_copies, swaps = {}, {}, {}, {}

    def dispatch(t, s):
        z_copies[t, s] = []
        for d in (1, 7, 2, 6, 3, 5, 4):
            to = lax.rem(z + d, NZ)
            copy = go(remote(src.at[t, s, to // 4], gat.at[t, s, x, z], gss.at[t, s, d], grs.at[t, s, d], at_z(to)))
            z_copies[t, s].append((d, copy))
        gat[t, s, x, z] = src[t, s, z // 4]

    def relay(t, s):
        def pass_on(block, d):
            slot = gat.at[t, s, x, block]
            return go(remote(slot, slot, xss.at[t, s, d], xrs.at[t, s, d], across))

        x_copies[t, s] = [pass_on(z, 0)]
        for d, arriving in z_copies[t, s]:
            arriving.wait_recv()
            x_copies[t, s].append(pass_on(lax.rem(z + NZ - d, NZ), d))

    def arrived(t, s):
        for copy in x_copies[t, s]:
            copy.wait_recv()

    def pre(t, s, line):
        rows = gat[t, s, line].reshape(NZ * 32, LANES)
        if s == 0:
            for k in range(2):
                got = pick([nn(rows, win[k, p * LANES:(p + 1) * LANES]) for p in range(3)])
                preo_a[t, line, :, k * 256:(k + 1) * 256] = fold(got)
        else:
            preo_b[t, line] = fold(pick([nt(rows, wout[:, p * LANES:(p + 1) * LANES]) for p in range(3)]))

    def swap(t, s):
        mine, theirs = ((preo_a, pret_a), (preo_b, pret_b))[s]
        i = 2 + 2 * t + s
        swaps[t, s] = go(remote(mine.at[t], theirs.at[t], twss.at[i], twrs.at[i], twin))

    def hidden(t, s, line):
        if s == 0:
            g = preo_a[t, line] + pret_a[t, line]
            return jnp.concatenate([
                jax.nn.silu(g[:, 256 * k:256 * k + 128]) * g[:, 256 * k + 128:256 * k + 256] for k in range(2)], axis=1)
        g = preo_b[t, line] + pret_b[t, line]
        cols = []
        for k in range(2):
            ab = spx[k, t, line].astype(f32)
            a, b = ab[:, :128], ab[:, 128:]
            q = jax.nn.sigmoid(a)
            gk = g[:, 128 * k:128 * k + 128]
            cols += [gk * b * q * (1.0 + a * (1.0 - q)), gk * a * q]
        return jnp.concatenate(cols, axis=1)

    def post(t, s, line, emit):
        parts = expand(hidden(t, s, line))

        @pl.loop(0, LANES // STEP)
        def _(n):
            total = None
            for p in range(3):
                cols = pl.ds(pl.multiple_of(p * LANES + n * STEP, STEP), STEP)
                if s == 0:
                    terms = [nn(parts[p], wout[:, cols])]
                else:
                    terms = [nt(parts[p][:, 256 * k:256 * k + 256], win[k, cols]) for k in range(2)]
                for term in terms:
                    total = term if total is None else total + term
            emit(n, total)

    def lanes(n):
        return pl.ds(pl.multiple_of(n * STEP, STEP), STEP)

    def chunk(t, s, n):
        return remote(obuf.at[t, s, :, lanes(n)], xr.at[t, s, :, lanes(n)], oss.at[t, s, n], ors.at[t, s, n], across)

    def give_across(t, s):
        swaps[t, s].wait_recv()

        def emit(n, total):
            obuf[t, s, :, lanes(n)] = total.astype(bf16)
            chunk(t, s, n).start()

        post(t, s, 1 - x, emit)

    def keep(t, s):
        def emit(n, total):
            own[s, :, lanes(n)] = total

        post(t, s, x, emit)

    def give_back(t, s):
        @pl.loop(0, LANES // STEP)
        def _(n):
            chunk(t, s, n).wait_recv()
            total = own[s, :, lanes(n)] + xr[t, s, :, lanes(n)].astype(f32)
            zb[t, s, :, :, :, lanes(n)] = total.astype(bf16).reshape(NZ, 2, 16, STEP)

        back_copies[t, s] = []
        for d in (4, 3, 5, 2, 6, 1, 7):
            to = lax.rem(z + d, NZ)
            back_copies[t, s].append(go(
                remote(zb.at[t, s, to], rz.at[t, s, z], zss.at[t, s, d], zrs.at[t, s, d], at_z(to))))
        rz[t, s, z] = zb[t, s, z]

    def finish(t, s):
        for copy in back_copies[t, s]:
            copy.wait_recv()
        for core in range(2):
            totals = []
            for e in range(2):
                total = rz[t, s, 4 * e, core].astype(f32)
                for i in range(1, 4):
                    total = total + rz[t, s, 4 * e + i, core].astype(f32)
                totals.append(total)
            added = jnp.dot(mt[t, s, core], jnp.concatenate(totals, axis=0), precision=lax.Precision.HIGHEST,
                            preferred_element_type=f32)
            fresh = src[t, s, :, core].reshape(32, LANES).astype(f32) + added
            nv[t, s, core] = fresh.astype(bf16).reshape(2, 16, LANES)

    def mixing():
        for copy in twin_tables:
            copy.wait_recv()
        for t in range(2):
            for s in range(2):
                for core, names, gains in ((c, ids, weights), (other, idt, wtt)):
                    choose, scaled, _, _ = tables(names[t, s], gains[t, s])
                    total = None
                    for a, b in zip(expand(choose, f32), expand(scaled, f32)):
                        term = lax.dot_general(a, b, (((1,), (1,)), ((), ())), precision=lax.Precision.HIGHEST,
                                               preferred_element_type=f32)
                        total = term if total is None else total + term
                    mt[t, s, core] = total

    def prepare(s):
        behind[s].wait_recv()
        bulk[s].wait_recv()
        touched = tables(rt2[s])[3][:1]
        parts = expand(tables(ids[1, s])[0] * (1.0 - touched))
        for half in range(2):
            base[s, half] = pack(parts, xb.at[s], half).astype(bf16)

    def pass_rows(s):
        return [go(remote(nv.at[0, s, core], nw.at[0, s, c], pss.at[1, s, i], prs.at[1, s, i], (me, twin)[i],
                          section(steps[s])))
                for i, core in enumerate((c, other))]

    def second_rows(s, arriving):
        for copy in arriving:
            copy.wait_recv()
        lone = expand(tables(rt2[s])[2])
        choose = expand(tables(ids[1, s])[0])
        mix = nt(choose[0], lone[0]) + nt(choose[1], lone[1]) + nt(choose[2], lone[2])
        mix = mix.astype(bf16)
        for half in range(2):
            rows = base[s, half].astype(f32) + nn(mix, nw[0, s, half].reshape(32, LANES))
            pk[1, s, half] = rows.astype(bf16).reshape(2, 16, LANES)
        copy = go(remote(pk.at[1, s, other], src.at[1, s, :, c], twss.at[6 + s], twrs.at[6 + s], twin))
        src[1, s, :, c] = pk[1, s, c]
        copy.wait_recv()

    def place(names, rows, old, new):
        _, _, lone, _ = tables(names)
        touched = tn(lone.astype(bf16), jnp.ones((16, 128), bf16))[:, :1] > 0.0
        parts = expand(lone)
        for half in range(2):
            for p, (off, width) in enumerate(PARTS):
                cols = slice(half * HALF + off, half * HALF + off + width)
                put = tn(parts[p], rows[half].reshape(32, LANES)[:, :width])
                new[:, cols] = jnp.where(touched, put, old[:, cols].astype(f32)).astype(bf16)

    def exchange_last(s):
        nw[1, s, c] = nv[1, s, c]
        return go(remote(nv.at[1, s, other], nw.at[1, s, c], twss.at[8 + s], twrs.at[8 + s], twin))

    for s in range(2):
        for copy in first_rows[s]:
            copy.wait_recv()
        dispatch(0, s)
    mixing()
    for t in range(2):
        relay(t, 0)
        if t == 0:
            for copy in local_copies:
                copy.wait()
            for copy in weight_copies:
                copy.wait_recv()
        pre(t, 0, x)
        relay(t, 1)
        arrived(t, 0)
        pre(t, 0, 1 - x)
        swap(t, 0)
        pre(t, 1, x)
        give_across(t, 0)
        keep(t, 0)
        arrived(t, 1)
        pre(t, 1, 1 - x)
        swap(t, 1)
        give_back(t, 0)
        give_across(t, 1)
        keep(t, 1)
        if t == 0:
            prepare(0)
        give_back(t, 1)
        if t == 0:
            prepare(1)
            finish(0, 0)
            passed = [pass_rows(0)]
            second_rows(0, passed[0])
            dispatch(1, 0)
            finish(0, 1)
            passed.append(pass_rows(1))
            second_rows(1, passed[1])
            dispatch(1, 1)
            for s in range(2):
                place(rt2[s], nw[0, s], xb.at[s], out.at[s])
        else:
            last = []
            for s in range(2):
                finish(1, s)
                last.append(exchange_last(s))
                if s == 0:
                    last[0].wait_recv()
                    place(ids[1, 0], nw[1, 0], out.at[0], out.at[0])
            last[1].wait_recv()
            place(ids[1, 1], nw[1, 1], out.at[1], out.at[1])

    for copy in started:
        copy.wait_send()
    for t in range(2):
        for s in range(2):
            @pl.loop(0, LANES // STEP)
            def _(n):
                chunk(t, s, n).wait_send()


def local(forward_in, grad_in, routes, gate_weights, saved_preact, gate_up, down_proj):
    bf16, f32 = jnp.bfloat16, jnp.float32
    tokens, width = forward_in.shape[1:]
    ids = jnp.transpose(routes[0], (0, 1, 3, 2))
    weights = jnp.transpose(gate_weights[0], (0, 1, 3, 2))
    stored = jnp.transpose(saved_preact[0, :, 0].reshape(2, NZ, 2, 2, CAP, 256), (0, 2, 1, 3, 4, 5))
    stored = jnp.pad(stored, ((0, 0), (0, 0), (0, 0), (0, 0), (0, 8 - CAP), (0, 0))).reshape(2, 2, 128, 256)
    vmem = pl.BlockSpec(memory_space=pltpu.VMEM)
    hbm = pl.BlockSpec(memory_space=pl.ANY)
    dma = pltpu.SemaphoreType.DMA
    out = pl.pallas_call(
        relay_kernel,
        out_shape=jax.ShapeDtypeStruct((2, tokens, width), bf16),
        in_specs=[hbm, hbm, vmem, vmem, vmem, hbm, hbm],
        out_specs=vmem,
        scratch_shapes=[
            pltpu.VMEM((2, tokens, width), bf16),
            pltpu.VMEM((2, tokens, width), bf16),
            pltpu.VMEM((2, 8, tokens), jnp.int32),
            pltpu.VMEM((2, 8, tokens), jnp.int32),
            pltpu.VMEM((2, 2, 8, tokens), jnp.int32),
            pltpu.VMEM((2, 2, 8, tokens), f32),
            pltpu.VMEM((2, 2, 2, 2, 16, LANES), bf16),
            pltpu.VMEM((2, 2, 2, 2, 16, LANES), bf16),
            pltpu.VMEM((2, 2, 2, NZ, 2, 16, LANES), bf16),
            pltpu.VMEM((2, 3 * LANES, 256), bf16),
            pltpu.VMEM((256, 3 * LANES), bf16),
            pltpu.VMEM((2, 2, 2, 128, 256), bf16),
            pltpu.VMEM((2, 2, 128, 512), f32),
            pltpu.VMEM((2, 2, 128, 512), f32),
            pltpu.VMEM((2, 2, 128, 256), f32),
            pltpu.VMEM((2, 2, 128, 256), f32),
            pltpu.VMEM((2, 2, 256, LANES), bf16),
            pltpu.VMEM((2, 2, 256, LANES), bf16),
            pltpu.VMEM((2, 256, LANES), f32),
            pltpu.VMEM((2, 2, NZ, 2, 16, LANES), bf16),
            pltpu.VMEM((2, 2, NZ, 2, 16, LANES), bf16),
            pltpu.VMEM((2, 2, 2, 32, 32), f32),
            pltpu.VMEM((2, 2, 2, 2, 16, LANES), bf16),
            pltpu.VMEM((2, 2, 2, 2, 16, LANES), bf16),
            pltpu.VMEM((2, 2, 32, LANES), bf16),
            dma((8,)),
            dma((7,)), dma((7,)),
            dma((2, 2)), dma((2, 2)),
            dma((2, 2, 2)), dma((2, 2, 2)),
            dma((2,)), dma((2,)),
            dma((10,)), dma((10,)),
            dma((2, 2, 8)), dma((2, 2, 8)),
            dma((2, 2, 8)), dma((2, 2, 8)),
            dma((2, 2, 5)), dma((2, 2, 5)),
            dma((2, 2, 8)), dma((2, 2, 8)),
        ],
        compiler_params=pltpu.CompilerParams(
            collective_id=0, has_side_effects=True, vmem_limit_bytes=56 * 2 ** 20),
        name="expert_relay",
    )(forward_in[0], grad_in[0], ids, weights, stored, gate_up[0, 0], down_proj[0, 0])
    return (out[0][None], out[1][None])


def solution(mesh):
    in_specs = (
        P("pp", "ep", None),
        P("pp", "ep", None),
        P("pp", None, None, "ep", None),
        P("pp", None, None, "ep", None),
        P("pp", None, "ep", None, None, None),
        P("pp", "ep", None, None),
        P("pp", "ep", None, None),
    )
    out_specs = (P("pp", "ep", None), P("pp", "ep", None))
    return jax.shard_map(local, mesh=mesh, in_specs=in_specs, out_specs=out_specs, check_vma=False)
```

time: 814 us -> 200 us (0.25)
  waiting for transfers between devices: 636 us -> 0 us
  Pallas kernels: 0 us -> 193 us
  starting transfers between devices: 63.6 us -> 0 us
  matrix products: 51.4 us -> 0 us
  local copies, waits for them, and re-layouts: 47.9 us -> 5.96 us
  other arithmetic: 12.3 us -> 0 us
    all_to_all x8 -> x0, waiting for transfers between devices: 368 us -> none  [the longest x4 227 us: return_sums(): lax.all_to_all(partial_value, 'ep', split_axis=0, concat_axis=0, tiled=True)]
    ppermute x4 -> x0, waiting for transfers between devices: 268 us -> none  [passed_along(): return lax.ppermute(value, axis, pairs)]
    pallas_call x0 -> x1, Pallas kernels: none -> 193 us  [local(): pl.pallas_call(relay_kernel, out_shape=jax.ShapeDtypeStruct((2, tokens, w...]
    all_to_all x8 -> x0, starting transfers between devices: 51.8 us -> none  [the longest x4 32.3 us: send_rows(): lax.all_to_all(outgoing, 'ep', split_axis=0, concat_axis=0, tiled=True)]
    dot_general x16 -> x0, matrix products: 51.4 us -> none  [the longest x4 21.9 us: spread_rows(): jnp.dot(combine, flat_totals, precision=lax.Precision.HIGHEST, preferred_...]
    reshape x8 -> x0, local copies, waits for them, and re-layouts: 36.7 us -> none  [the longest x2 9.23 us: expert_backward(): flat_rows = routed.reshape(sources * capacity, model_width)]
    ppermute x4 -> x0, starting transfers between devices: 11.7 us -> none  [passed_along(): return lax.ppermute(value, axis, pairs)]
    reduce_sum x7 -> x0, other arithmetic: 11.5 us -> none  [the longest x4 11.4 us: return_sums(): jnp.sum(returned.astype(jnp.float32).reshape(EXP_SEC, split_ways, capacit...]
  transfers between devices with their start and end apart: 12 -> 0, of which waited for: 10 -> 0; matrix products, arithmetic and copies ran while one was open for 11% -> 0% of each run, Pallas kernels for 0% -> 0%
where the time goes in v2:
time: 200 us; the launch traced here: 199 us
  Pallas kernels  193 us (96%)
  local copies, waits for them, and re-layouts  5.96 us (3%)
    pallas_call x1, Pallas kernels, local(): pl.pallas_call(relay_kernel, out_shape=jax.ShapeDtypeStruct((2, tokens, w...  193 us
    slice x1, local copies, waits for them, and re-layouts, local(): return (out[0][None], out[1][None])  4.12 us

profile of v2, /device:TPU:1, one launch (start us, length us, event | category | flops | bytes accessed | tf_op | source)
XLA Modules:
  0.0 199.3 jit_solution(239882646896310815)
XLA Ops:
  0.6 1.0 reshape_squeeze.3
  1.6 0.1 copy.11
  1.7 0.8 pad.4
  2.5 192.7 %expert_relay.1 = bf16[2,128,7168]{2,1,0:T(8,128)(2,1)} custom-call(bf16[128,7168]{1,0:T(8,128)(2,1)} %bitcast.19, bf16[128,7168]{1,0:T(8,128)(2,1)} %bitcast.20, s32[2,2,8,128]{3,2,1,0:T(8,128)} %bitcast.24, f32[2,2,8,128]{3,2,1,0:T(8,128)} %bitcast.25, bf16[2,2,128,256]{3,2,1,0:T(8,128)(2,1)} %bitcast.22, bf16[7168,256]{1,0:T(8,128)(2,1)} %bitcast.18, ...), custom_call_target="tpu_custom_call" | custom-call | tf_op jit(solution)/shard_map/expert_relay/pallas_call | solution.py:438
  195.2 4.1 %fusion = (bf16[1,128,7168]{2,1,0:T(8,128)(2,1)}, bf16[1,128,7168]{2,1,0:T(8,128)(2,1)}) fusion(bf16[2,128,7168]{2,1,0:T(8,128)(2,1)} %expert_relay.1), kind=kLoop, calls=%fused_computation.1 | loop fusion | bytes 7340032 | tf_op jit(solution)/shard_map/slice | solution.py:484

commit v3 on v2

v3 whole, which is shorter than its diff:
```python
import functools

import jax
import jax.numpy as jnp
from jax import lax
from jax.experimental import pallas as pl
from jax.experimental.pallas import tpu as pltpu
from jax.sharding import PartitionSpec as P

EXP_SEC = 2
SEGMENTS = 2
CAP = 5
MESH = pl.DeviceIdType.MESH

HALF = 3584
LANES = 1152
REST = 3456
STEP = 384
NZ = 8


def row_in(rows, group):
    return lax.rem(lax.broadcasted_iota(jnp.int32, (rows, 1), 0), group)


def fold(parts, rests):
    rows, n = parts[0].shape
    size = rows // 2
    r = row_in(rows, 16)
    second = (r >= 8) & (r < 13)
    third = ((r >= 5) & (r < 8)) | (r >= 13)
    t = jnp.where(second, parts[1], jnp.where(third, parts[2], parts[0])).reshape(rows // 16, 16, n)
    a = t[:, :8].reshape(size, n)
    b = t[:, 8:].reshape(size, n)
    r = row_in(size, 8)
    low = jnp.where(r < 3, pltpu.roll(a, size - 5, 0), pltpu.roll(b, size - 2, 0))
    total = a + b + low
    for i, rest in enumerate(rests):
        rest = rest.reshape(rows // 16, 16, n)[:, 8:].reshape(size, n)
        total = total + jnp.where(r == i, pltpu.roll(rest, size - (7 - i), 0), 0.0)
    return jnp.where(r < CAP, total, 0.0)


def expand(h, dtype=jnp.bfloat16):
    rows, n = h.shape
    r = row_in(rows, 8)
    first = jnp.where(r < CAP, h, 0.0)
    third_a = jnp.where(r >= 5, pltpu.roll(h, 5, 0), 0.0)
    third_b = jnp.where((r == 5) | (r == 6), pltpu.roll(h, 2, 0), 0.0)
    none = jnp.zeros_like(first)

    def both(a, b):
        a, b = a.reshape(rows // 8, 8, n), b.reshape(rows // 8, 8, n)
        return jnp.concatenate([a, b], axis=1).reshape(rows * 2, n).astype(dtype)

    rests = [both(none, jnp.where(r == 7, pltpu.roll(h, 7 - i, 0), 0.0)) for i in range(CAP)]
    return [both(first, none), both(none, first), both(third_a, third_b)], rests


def nt(a, b):
    return lax.dot_general(a, b, (((1,), (1,)), ((), ())), preferred_element_type=jnp.float32)


def tn(a, b):
    return lax.dot_general(a, b, (((0,), (0,)), ((), ())), preferred_element_type=jnp.float32)


def nn(a, b):
    return jnp.dot(a, b, preferred_element_type=jnp.float32)


def tables(ids, weights=None):
    tokens = ids.shape[1]
    before = lax.broadcasted_iota(jnp.int32, (tokens, tokens), 0) <= lax.broadcasted_iota(jnp.int32, (tokens, tokens), 1)
    before = before.astype(jnp.float32).astype(jnp.bfloat16)
    place = lax.broadcasted_iota(jnp.int32, (8, tokens), 0).astype(jnp.float32)
    choose, scaled, lone, member = [], [], [], []
    for e in range(EXP_SEC):
        hit = ids == e
        named = jnp.sum(hit.astype(jnp.float32), axis=0, keepdims=True) + jnp.zeros((8, tokens), jnp.float32)
        rank = nn(named.astype(jnp.bfloat16), before)
        slot = jnp.where((named > 0.0) & (rank - 1.0 == place) & (place < CAP), 1.0, 0.0)
        choose.append(slot)
        lone.append(slot if e == 0 else slot * (1.0 - member[0]))
        member.append(named)
        if weights is not None:
            scaled.append(slot * jnp.sum(jnp.where(hit, weights, 0.0), axis=0, keepdims=True))
    choose, lone = jnp.concatenate(choose, axis=0), jnp.concatenate(lone, axis=0)
    scaled = jnp.concatenate(scaled, axis=0) if weights is not None else None
    touched = jnp.maximum(member[0], member[1])
    return choose, scaled, lone, touched


def part_cols(half, p):
    return slice(half * HALF + p * LANES, half * HALF + (p + 1) * LANES)


def rest_cols(half):
    return slice(half * HALF + REST, (half + 1) * HALF)


def in_lanes(rests):
    blank = jnp.zeros((rests[0].shape[0], LANES - 128 * CAP), jnp.float32)
    return jnp.concatenate(rests + [blank], axis=1)


def pack(choose, tokens, half):
    parts, rests = expand(choose)
    wide = in_lanes([nn(rest, tokens[:, rest_cols(half)]) for rest in rests])
    for p in range(3):
        wide = wide + nn(parts[p], tokens[:, part_cols(half, p)])
    return wide


def exact(a, b):
    return jnp.dot(a, b, precision=lax.Precision.HIGHEST, preferred_element_type=jnp.float32)


def mixer(left, right):
    def one(a, b):
        return lax.dot_general(a, b, (((1,), (1,)), ((), ())), precision=lax.Precision.HIGHEST,
                               preferred_element_type=jnp.float32)

    lefts, rights = expand(left, jnp.float32)[0], expand(right, jnp.float32)[0]
    return one(lefts[0], rights[0]) + one(lefts[1], rights[1]) + one(lefts[2], rights[2]), one(left, right)


def mixed(by_row, by_slot, rows):
    r = row_in(16, 8)
    last = jnp.concatenate([rows[8:16], rows[24:32]], axis=0)
    slots = jnp.zeros((16, 128), jnp.float32)
    for i in range(CAP):
        slots = jnp.where(r == i, pltpu.roll(last[:, 128 * i:128 * i + 128], 16 - (7 - i), 0), slots)
    slots = exact(by_slot, slots)
    none = jnp.zeros((8, 128), jnp.float32)
    rests = []
    for i in range(CAP):
        rest = jnp.where(r == 7, pltpu.roll(slots, 7 - i, 0), 0.0)
        rests.append(jnp.concatenate([none, rest[:8], none, rest[8:]], axis=0))
    return exact(by_row, rows) + in_lanes(rests)


def relay_kernel(x_in, y_in, ids, weights, stored, w_in, w_out, out0, out1, xv, xb, rt0, rt2, idt, wtt, pk, src, gat, win, wout,
                 spx, preo_a, pret_a, preo_b, pret_b, obuf, xr, own, zb, rz, mt, ms, nv, nw, base, lsem, wss, wrs, tss, trs,
                 pss, prs, bss, brs, twss, twrs, gss, grs, xss, xrs, oss, ors, zss, zrs):
    me = lax.axis_index("ep")
    pp = lax.axis_index("pp")
    n_pp = lax.axis_size("pp")
    z = me // 4
    x = lax.rem(me // 2, 2)
    c = lax.rem(me, 2)
    other = 1 - c
    twin = z * 4 + x * 2 + other
    across = z * 4 + (1 - x) * 2 + c
    steps = (1, n_pp - 1)
    bf16, f32 = jnp.bfloat16, jnp.float32

    def at_z(zz):
        return zz * 4 + x * 2 + c

    def remote(a, b, ss, rs, device, section=None):
        where = {"ep": device} if section is None else {"pp": section, "ep": device}
        return pltpu.make_async_remote_copy(
            src_ref=a, dst_ref=b, send_sem=ss, recv_sem=rs, device_id=where, device_id_type=MESH)

    def section(hops):
        return lax.rem(pp + hops, n_pp)

    partners = [{"ep": twin}, {"ep": across}] + [{"ep": at_z(lax.rem(z + d, NZ))} for d in range(1, NZ)]
    for hops in (1, n_pp - 1):
        partners += [{"pp": section(hops), "ep": me}, {"pp": section(hops), "ep": twin}]
    for hops in (2, n_pp - 2):
        partners.append({"pp": section(hops), "ep": me})
    locals_x = []
    for s, tokens in enumerate((x_in, y_in)):
        copy = pltpu.make_async_copy(tokens, xv.at[s], lsem.at[2 + s])
        copy.start()
        locals_x.append(copy)
    barrier = pltpu.get_barrier_semaphore()
    for device in partners:
        pl.semaphore_signal(barrier, inc=1, device_id=device, device_id_type=MESH)
    pl.semaphore_wait(barrier, len(partners))

    started = []

    def go(copy):
        copy.start()
        started.append(copy)
        return copy

    ahead, behind = [], []
    for s in range(2):
        ahead.append(go(remote(ids.at[0, s], rt0.at[s], tss.at[s, 0], trs.at[s, 0], me, section(n_pp - steps[s]))))
    for s in range(2):
        behind.append(go(remote(ids.at[0, s], rt2.at[s], tss.at[s, 1], trs.at[s, 1], me, section(steps[s]))))
    twin_tables = [go(remote(ids, idt, twss.at[0], twrs.at[0], twin)),
                   go(remote(weights, wtt, twss.at[1], twrs.at[1], twin))]

    weight_copies, local_copies = [], []
    mine = pl.ds(pl.multiple_of(c * HALF, 128), HALF)
    theirs = pl.ds(pl.multiple_of(other * HALF, 128), HALF)
    down = pl.ds(pl.multiple_of(c * 128, 128), 128)
    pairs = ((w_in.at[mine], w_in.at[theirs], win.at[c]), (w_out.at[:, mine], w_out.at[:, theirs], wout.at[down]))
    for k, (keep_part, give_part, slot) in enumerate(pairs):
        weight_copies.append(go(remote(give_part, slot, wss.at[k], wrs.at[k], twin)))
        copy = pltpu.make_async_copy(keep_part, slot, lsem.at[k])
        copy.start()
        local_copies.append(copy)
    weight_copies.append(go(remote(stored, spx.at[c], wss.at[2], wrs.at[2], twin)))
    spx[c] = stored[...]

    first_rows = []
    for s in range(2):
        ahead[s].wait_recv()
        locals_x[s].wait()
        choose = tables(rt0[s])[0]
        for half in range(2):
            pk[0, s, half] = pack(choose, xv.at[s], half).astype(bf16).reshape(2, 16, LANES)
        first_rows.append([
            go(remote(pk.at[0, s, half], src.at[0, s, :, c], pss.at[0, s, i], prs.at[0, s, i],
                      (me, twin)[i], section(steps[s])))
            for i, half in enumerate((c, other))])

    bulk = [go(remote(tokens, xb.at[s], bss.at[s], brs.at[s], me, section(2 * steps[s] if s == 0 else n_pp - 2)))
            for s, tokens in enumerate((x_in, y_in))]

    z_copies, x_copies, swaps = {}, {}, {}

    def dispatch(t, s):
        z_copies[t, s] = {}
        for d in (4, 3, 5, 2, 6, 1, 7):
            to = lax.rem(z + d, NZ)
            z_copies[t, s][d] = go(
                remote(src.at[t, s, to // 4], gat.at[t, s, x, z], gss.at[t, s, d], grs.at[t, s, d], at_z(to)))
        gat[t, s, x, z] = src[t, s, z // 4]

    def pass_across(t, s, d):
        slot = gat.at[t, s, x, lax.rem(z + NZ - d, NZ)]
        x_copies[t, s].append(go(remote(slot, slot, xss.at[t, s, d], xrs.at[t, s, d], across)))

    def relay_some(t, s, *hops):
        for d in hops:
            z_copies[t, s][d].wait_recv()
            pass_across(t, s, d)

    def relay_first(t, s):
        x_copies[t, s] = []
        pass_across(t, s, 0)
        relay_some(t, s, 3, 5)
        relay_some(t, s, 2, 6)

    def relay_last(t, s):
        relay_some(t, s, 1, 7, 4)

    def arrived(t, s):
        for copy in x_copies[t, s]:
            copy.wait_recv()

    def pre(t, s, line):
        rows = gat[t, s, line].reshape(NZ * 32, LANES)
        for k in range(2 - s):
            def product(lhs, cols):
                return nn(lhs, win[k, cols]) if s == 0 else nt(lhs, wout[:, cols])

            got = fold([product(rows, part_cols(0, p)) for p in range(3)],
                       [product(rows[:, 128 * i:128 * i + 128], rest_cols(0)) for i in range(CAP)])
            if s == 0:
                preo_a[t, line, :, k * 256:(k + 1) * 256] = got
            else:
                preo_b[t, line] = got

    def swap(t, s):
        mine, theirs = ((preo_a, pret_a), (preo_b, pret_b))[s]
        i = 2 + 2 * t + s
        swaps[t, s] = go(remote(mine.at[t], theirs.at[t], twss.at[i], twrs.at[i], twin))

    def hidden(t, s, line):
        if s == 0:
            g = preo_a[t, line] + pret_a[t, line]
            return jnp.concatenate([
                jax.nn.silu(g[:, 256 * k:256 * k + 128]) * g[:, 256 * k + 128:256 * k + 256] for k in range(2)], axis=1)
        g = preo_b[t, line] + pret_b[t, line]
        cols = []
        for k in range(2):
            ab = spx[k, t, line].astype(f32)
            a, b = ab[:, :128], ab[:, 128:]
            q = jax.nn.sigmoid(a)
            gk = g[:, 128 * k:128 * k + 128]
            cols += [gk * b * q * (1.0 + a * (1.0 - q)), gk * a * q]
        return jnp.concatenate(cols, axis=1)

    def post(t, s, line, emit):
        parts, rests = expand(hidden(t, s, line))

        def product(lhs, cols):
            if s == 0:
                return nn(lhs, wout[:, cols])
            return nt(lhs[:, :256], win[0, cols]) + nt(lhs[:, 256:], win[1, cols])

        for n in range(LANES // STEP):
            total = None
            for p in range(3):
                term = product(parts[p], slice(p * LANES + n * STEP, p * LANES + (n + 1) * STEP))
                total = term if total is None else total + term
            here = rests[3 * n:3 * n + 3]
            if here:
                here = [product(rest, rest_cols(0)) for rest in here]
                here += [jnp.zeros_like(here[0])] * (3 - len(here))
                total = total + jnp.concatenate(here, axis=1)
            emit(n, total)

    def lanes(n):
        return pl.ds(n * STEP if isinstance(n, int) else pl.multiple_of(n * STEP, STEP), STEP)

    def chunk(t, s, n):
        return remote(obuf.at[t, s, :, lanes(n)], xr.at[t, s, :, lanes(n)], oss.at[t, s, n], ors.at[t, s, n], across)

    def give_across(t, s, now):
        swaps[t, s].wait_recv()

        def emit(n, total):
            obuf[t, s, :, lanes(n)] = total.astype(bf16)
            if now:
                chunk(t, s, n).start()

        post(t, s, 1 - x, emit)

    def send_across(t, s):
        for n in range(LANES // STEP):
            chunk(t, s, n).start()

    def keep(t, s):
        def emit(n, total):
            own[s, :, lanes(n)] = total

        post(t, s, x, emit)

    def onward(t, s, d):
        to = lax.rem(z + d, NZ)
        return remote(zb.at[t, s, to], rz.at[t, s, z], zss.at[t, s, d], zrs.at[t, s, d], at_z(to))

    def give_back(t, s):
        @pl.loop(0, LANES // STEP)
        def _(n):
            chunk(t, s, n).wait_recv()
            total = own[s, :, lanes(n)] + xr[t, s, :, lanes(n)].astype(f32)
            zb[t, s, :, :, :, lanes(n)] = total.astype(bf16).reshape(NZ, 2, 16, STEP)

        for d in (4, 3, 5, 2, 6, 1, 7):
            onward(t, s, d).start()
        rz[t, s, z] = zb[t, s, z]

    def merge(t, s):
        pass

    def finish(t, s):
        for d in range(1, NZ):
            onward(t, s, d).wait_recv()

        for core in range(2):
            totals = []
            for e in range(2):
                total = rz[t, s, 4 * e, core].astype(f32)
                for i in range(1, 4):
                    total = total + rz[t, s, 4 * e + i, core].astype(f32)
                totals.append(total)
            added = mixed(mt[t, s, core], ms[t, s, core], jnp.concatenate(totals, axis=0))
            fresh = src[t, s, :, core].reshape(32, LANES).astype(f32) + added
            nv[t, s, core] = fresh.astype(bf16).reshape(2, 16, LANES)

    def mixing(t):
        if t == 0:
            for copy in twin_tables:
                copy.wait_recv()
        for s in range(2):
            for core, names, gains in ((c, ids, weights), (other, idt, wtt)):
                choose, scaled, _, _ = tables(names[t, s], gains[t, s])
                mt[t, s, core], ms[t, s, core] = mixer(choose, scaled)

    def prepare(s):
        behind[s].wait_recv()
        bulk[s].wait_recv()
        touched = tables(rt2[s])[3][:1]
        choose = tables(ids[1, s])[0] * (1.0 - touched)
        for half in range(2):
            base[s, half] = pack(choose, xb.at[s], half).astype(bf16)

    def pass_rows(s):
        return [go(remote(nv.at[0, s, core], nw.at[0, s, c], pss.at[1, s, i], prs.at[1, s, i], (me, twin)[i],
                          section(steps[s])))
                for i, core in enumerate((c, other))]

    def second_rows(s, arriving):
        for copy in arriving:
            copy.wait_recv()
        by_row, by_slot = mixer(tables(ids[1, s])[0], tables(rt2[s])[2])
        for half in range(2):
            rows = base[s, half].astype(f32) + mixed(by_row, by_slot, nw[0, s, half].reshape(32, LANES).astype(f32))
            pk[1, s, half] = rows.astype(bf16).reshape(2, 16, LANES)
        copy = go(remote(pk.at[1, s, other], src.at[1, s, :, c], twss.at[6 + s], twrs.at[6 + s], twin))
        src[1, s, :, c] = pk[1, s, c]
        copy.wait_recv()

    def place(names, rows, old, new):
        _, _, lone, _ = tables(names)
        touched = tn(lone.astype(bf16), jnp.ones((16, 128), bf16))[:, :1] > 0.0
        parts, rests = expand(lone)
        for half in range(2):
            fresh = rows[half].reshape(32, LANES)
            for p in range(3):
                cols = part_cols(half, p)
                new[:, cols] = jnp.where(touched, tn(parts[p], fresh), old[:, cols].astype(f32)).astype(bf16)
            cols = rest_cols(half)
            put = None
            for i in range(CAP):
                term = tn(rests[i], fresh[:, 128 * i:128 * i + 128])
                put = term if put is None else put + term
            new[:, cols] = jnp.where(touched, put, old[:, cols].astype(f32)).astype(bf16)

    def exchange_last(s):
        nw[1, s, c] = nv[1, s, c]
        return go(remote(nv.at[1, s, other], nw.at[1, s, c], twss.at[8 + s], twrs.at[8 + s], twin))

    for s in range(2):
        for copy in first_rows[s]:
            copy.wait_recv()
        dispatch(0, s)
    for t in range(2):
        relay_first(t, 0)
        relay_last(t, 0)
        if t == 0:
            for copy in local_copies:
                copy.wait()
            for copy in weight_copies:
                copy.wait_recv()
        pre(t, 0, x)
        relay_first(t, 1)
        relay_last(t, 1)
        arrived(t, 0)
        pre(t, 0, 1 - x)
        swap(t, 0)
        pre(t, 1, x)
        give_across(t, 0, True)
        keep(t, 0)
        arrived(t, 1)
        pre(t, 1, 1 - x)
        swap(t, 1)
        mixing(t)
        give_across(t, 1, True)
        give_back(t, 0)
        keep(t, 1)
        if t == 0:
            prepare(0)
        merge(t, 0)
        give_back(t, 1)
        merge(t, 1)
        if t == 0:
            prepare(1)
            finish(0, 0)
            passed = pass_rows(0)
            second_rows(0, passed)
            dispatch(1, 0)
            finish(0, 1)
            passed = pass_rows(1)
            second_rows(1, passed)
            dispatch(1, 1)
    for s, half_done in enumerate((out0, out1)):
        place(rt2[s], nw[0, s], xb.at[s], half_done)
    finish(1, 0)
    last = exchange_last(0)
    last.wait_recv()
    place(ids[1, 0], nw[1, 0], out0, out0)
    finish(1, 1)
    exchange_last(1).wait_recv()
    place(ids[1, 1], nw[1, 1], out1, out1)

    for copy in started:
        copy.wait_send()
    for t in range(2):
        for s in range(2):
            @pl.loop(0, LANES // STEP)
            def _(n):
                chunk(t, s, n).wait_send()

            for d in range(1, NZ):
                onward(t, s, d).wait_send()


def local(forward_in, grad_in, routes, gate_weights, saved_preact, gate_up, down_proj):
    bf16, f32 = jnp.bfloat16, jnp.float32
    tokens, width = forward_in.shape[1:]
    ids = jnp.transpose(routes[0], (0, 1, 3, 2))
    weights = jnp.transpose(gate_weights[0], (0, 1, 3, 2))
    stored = jnp.transpose(saved_preact[0, :, 0].reshape(2, NZ, 2, 2, CAP, 256), (0, 2, 1, 3, 4, 5))
    stored = jnp.pad(stored, ((0, 0), (0, 0), (0, 0), (0, 0), (0, 8 - CAP), (0, 0))).reshape(2, 2, 128, 256)
    vmem = pl.BlockSpec(memory_space=pltpu.VMEM)
    hbm = pl.BlockSpec(memory_space=pl.ANY)
    dma = pltpu.SemaphoreType.DMA
    out = pl.pallas_call(
        relay_kernel,
        out_shape=(jax.ShapeDtypeStruct((tokens, width), bf16),) * 2,
        in_specs=[hbm, hbm, vmem, vmem, vmem, hbm, hbm],
        out_specs=(vmem, vmem),
        scratch_shapes=[
            pltpu.VMEM((2, tokens, width), bf16),
            pltpu.VMEM((2, tokens, width), bf16),
            pltpu.VMEM((2, 8, tokens), jnp.int32),
            pltpu.VMEM((2, 8, tokens), jnp.int32),
            pltpu.VMEM((2, 2, 8, tokens), jnp.int32),
            pltpu.VMEM((2, 2, 8, tokens), f32),
            pltpu.VMEM((2, 2, 2, 2, 16, LANES), bf16),
            pltpu.VMEM((2, 2, 2, 2, 16, LANES), bf16),
            pltpu.VMEM((2, 2, 2, NZ, 2, 16, LANES), bf16),
            pltpu.VMEM((2, HALF, 256), bf16),
            pltpu.VMEM((256, HALF), bf16),
            pltpu.VMEM((2, 2, 2, 128, 256), bf16),
            pltpu.VMEM((2, 2, 128, 512), f32),
            pltpu.VMEM((2, 2, 128, 512), f32),
            pltpu.VMEM((2, 2, 128, 256), f32),
            pltpu.VMEM((2, 2, 128, 256), f32),
            pltpu.VMEM((2, 2, 256, LANES), bf16),
            pltpu.VMEM((2, 2, 256, LANES), bf16),
            pltpu.VMEM((2, 256, LANES), f32),
            pltpu.VMEM((2, 2, NZ, 2, 16, LANES), bf16),
            pltpu.VMEM((2, 2, NZ, 2, 16, LANES), bf16),
            pltpu.VMEM((2, 2, 2, 32, 32), f32),
            pltpu.VMEM((2, 2, 2, 16, 16), f32),
            pltpu.VMEM((2, 2, 2, 2, 16, LANES), bf16),
            pltpu.VMEM((2, 2, 2, 2, 16, LANES), bf16),
            pltpu.VMEM((2, 2, 32, LANES), bf16),
            dma((4,)),
            dma((3,)), dma((3,)),
            dma((2, 2)), dma((2, 2)),
            dma((2, 2, 2)), dma((2, 2, 2)),
            dma((2,)), dma((2,)),
            dma((10,)), dma((10,)),
            dma((2, 2, 8)), dma((2, 2, 8)),
            dma((2, 2, 8)), dma((2, 2, 8)),
            dma((2, 2, 3)), dma((2, 2, 3)),
            dma((2, 2, 8)), dma((2, 2, 8)),
        ],
        compiler_params=pltpu.CompilerParams(
            collective_id=0, has_side_effects=True, vmem_limit_bytes=56 * 2 ** 20),
        name="expert_relay",
    )(forward_in[0], grad_in[0], ids, weights, stored, gate_up[0, 0], down_proj[0, 0])
    return (out[0][None], out[1][None])


def solution(mesh):
    in_specs = (
        P("pp", "ep", None),
        P("pp", "ep", None),
        P("pp", None, None, "ep", None),
        P("pp", None, None, "ep", None),
        P("pp", None, "ep", None, None, None),
        P("pp", "ep", None, None),
        P("pp", "ep", None, None),
    )
    out_specs = (P("pp", "ep", None), P("pp", "ep", None))
    return jax.shard_map(local, mesh=mesh, in_specs=in_specs, out_specs=out_specs, check_vma=False)
```

time: 200 us -> 188 us (0.940)
  Pallas kernels: 193 us -> 181 us
    pallas_call x1, Pallas kernels: 193 us -> 181 us  [local(): pl.pallas_call(relay_kernel, out_shape=(jax.ShapeDtypeStruct((tokens, wid...]
    unnamed x0 -> x4, local copies, waits for them, and re-layouts: none -> 4.21 us
    slice x1 -> x0, local copies, waits for them, and re-layouts: 4.12 us -> none  [local(): return (out[0][None], out[1][None])]
where the time goes in v3:
time: 188 us
  Pallas kernels  181 us (96%)
  local copies, waits for them, and re-layouts  6.05 us (3%)
    pallas_call x1, Pallas kernels, local(): pl.pallas_call(relay_kernel, out_shape=(jax.ShapeDtypeStruct((tokens, wid...  181 us
    unnamed x4, local copies, waits for them, and re-layouts  4.21 us

profile of v3, /device:TPU:1, one launch (start us, length us, event | category | flops | bytes accessed | tf_op | source)
XLA Modules:
  0.0 187.9 jit_solution(13904958976665527148)
XLA Ops:
  0.6 1.0 reshape_squeeze.3
  1.6 0.1 copy.11
  1.7 0.8 pad.4
  2.5 181.2 %expert_relay.1 = (bf16[128,7168]{1,0:T(8,128)(2,1)}, bf16[128,7168]{1,0:T(8,128)(2,1)}) custom-call(bf16[128,7168]{1,0:T(8,128)(2,1)} %bitcast.21, bf16[128,7168]{1,0:T(8,128)(2,1)} %bitcast.22, s32[2,2,8,128]{3,2,1,0:T(8,128)} %bitcast.28, f32[2,2,8,128]{3,2,1,0:T(8,128)} %bitcast.29, bf16[2,2,128,256]{3,2,1,0:T(8,128)(2,1)} %bitcast.26, ...), custom_call_target="tpu_custom_call" | custom-call | tf_op jit(solution)/shard_map/expert_relay/pallas_call | solution.py:499
  183.7 0.0 copy-start
  183.7 3.0 %copy.14 = bf16[1,128,7168]{2,1,0:T(8,128)(2,1)} copy(bf16[1,128,7168]{2,1,0:T(8,128)(2,1)} %bitcast.25) | data formatting | bytes 3670016
  186.7 0.0 copy-done
  186.7 1.2 copy.15
Async XLA Ops:
  183.7 3.0 %copy-start = (bf16[128,7168]{1,0:T(8,128)(2,1)S(1)}, bf16[128,7168]{1,0:T(8,128)(2,1)}, u32[]{:S(2)}) copy-start(bf16[128,7168]{1,0:T(8,128)(2,1)} %get-tuple-element.5) | copy-start | bytes 5505028
